TPU v7x, 32 devices: a whole 2x2x4 slice. The times are simulated.
32 devices in a mesh: exp: 8 (over z, x), hid: 4 (over y, core).
Axes of the slice: x: 2, y: 2, z: 4, core: 2. Of those that a mesh axis runs over, the one named last changes fastest.
Arguments:
- tokens: bfloat16 [8192, 1024], P('exp'), may hold values from -6 to 6
- segment_ids: int32 [8, 1024], P('exp'), may hold values from 0 to 3, never falling along the last dimension, each value on 1 to 682 neighbouring positions
- routes: int32 [8192, 8], P('exp'), may hold values from 0 to 31, all different within a row
- norm1_gain: float32 [1024], P('exp'), may hold values from 0.5 to 1.5
- norm2_gain: float32 [1024], P('exp'), may hold values from 0.5 to 1.5
- query_weight: float32 [1024, 1024], P('exp', 'hid'), may hold values from -0.1875 to 0.1875
- key_matrix: float32 [1024, 512], P('exp', 'hid'), may hold values from -0.1875 to 0.1875
- value_matrix: float32 [1024, 512], P('exp', 'hid'), may hold values from -0.1875 to 0.1875
- out_weight: float32 [1024, 1024], P('exp', 'hid'), may hold values from -0.75 to 0.75
- router_weight: float32 [1024, 32], P('exp'), may hold values from -0.09375 to 0.09375
- gate_weight: float32 [32, 1024, 512], P('exp', None, 'hid'), may hold values from -0.1875 to 0.1875
- up_weight: float32 [32, 1024, 512], P('exp', None, 'hid'), may hold values from -0.1875 to 0.1875
- down_weight: float32 [32, 512, 1024], P('exp', 'hid'), may hold values from -1 to 1
- out_grad: bfloat16 [8192, 1024], P('exp', 'hid'), may hold values from -6 to 6
Outputs:
- layer_out: bfloat16 [8192, 1024], P('exp', 'hid')
- input_grad: float32 [8192, 1024], P('exp')
- norm1_gain_grad: float32 [1024], P('exp')
- norm2_gain_grad: float32 [1024], P('exp')
- query_weight_grad: float32 [1024, 1024], P('exp', 'hid')
- key_weight_grad: float32 [1024, 512], P('exp', 'hid')
- value_weight_grad: float32 [1024, 512], P('exp', 'hid')
- out_weight_grad: float32 [1024, 1024], P('exp', 'hid')
- router_weight_grad: float32 [1024, 32], P('exp')
- gate_weight_grad: float32 [32, 1024, 512], P('exp', None, 'hid')
- up_weight_grad: float32 [32, 1024, 512], P('exp', None, 'hid')
- down_weight_grad: float32 [32, 512, 1024], P('exp', 'hid')
Inputs may be any that keep to these rules, and one draw needn't show every extreme that they name: `routes`: each token names 8 different experts. `segment_ids`: within a row ids never fall; a document has at most 682 tokens and one has exactly that many.
All inputs are finite; a program needn't handle non-finite values.
Results may differ from a plain program's by a relative error of at most 0.023.
Values may be sent and summed in bfloat16 or wider, within the bound.
A program may use at most 384 MiB of HBM per device.

v0:
```python
import jax
import jax.numpy as jnp
from jax import lax
from jax.sharding import PartitionSpec as P

HEAD_DIM = 64
SEGS = 4


EPSILON = 1e-05
ROPE_BASE = 10000.0
NEG_FILL = -1e30


def rms_scale(values_in):
    return lax.rsqrt(jnp.mean(values_in * values_in, axis=-1, keepdims=True) + EPSILON)


def norm_back(grad_normed, inputs, scale_rows, gain_row):
    weighted = grad_normed * gain_row[None, :]
    return scale_rows * weighted - inputs * scale_rows**3 * jnp.mean(
        weighted * inputs, axis=-1, keepdims=True
    )


def positions_of(segments, seg_count):
    same = segments[:, None] == jnp.arange(seg_count, dtype=jnp.int32)[None, :]
    counts = jnp.sum(same.astype(jnp.int32), axis=0)
    starts = jnp.cumsum(counts) - counts
    begin = jnp.sum(jnp.where(same, starts[None, :], 0), axis=1)
    return jnp.arange(segments.shape[0], dtype=jnp.int32) - begin


def rope_tables(positions, head_size):
    half = head_size // 2
    freqs = ROPE_BASE ** (-(jnp.arange(half, dtype=jnp.float32) * 2.0 / head_size))
    angles = positions.astype(jnp.float32)[:, None] * freqs[None, :]
    return (jnp.cos(angles)[:, None, :], jnp.sin(angles)[:, None, :])


def rotate(values_in, cosine, sine):
    half = values_in.shape[-1] // 2
    first = values_in[..., :half]
    second = values_in[..., half:]
    return jnp.concatenate(
        [first * cosine - second * sine, second * cosine + first * sine], axis=-1
    )


def rotate_back(grads_in, cosine, sine):
    half = grads_in.shape[-1] // 2
    first = grads_in[..., :half]
    second = grads_in[..., half:]
    return jnp.concatenate(
        [first * cosine + second * sine, second * cosine - first * sine], axis=-1
    )


def slot_tables(row_routes, expert_count, capacity):
    token_count = row_routes.shape[0]
    chosen = row_routes[:, :, None] == jnp.arange(expert_count, dtype=jnp.int32)[None, None, :]
    chosen_int = chosen.astype(jnp.int32)
    per_token = jnp.sum(chosen_int, axis=1)
    before = jnp.cumsum(per_token, axis=0) - per_token
    rank = jnp.sum(chosen_int * before[:, None, :], axis=2)
    pair_slot = jnp.where(rank < capacity, row_routes * capacity + rank, expert_count * capacity)
    owners = jnp.broadcast_to(jnp.arange(token_count, dtype=jnp.int32)[:, None], row_routes.shape)
    source = jnp.full((expert_count * capacity + 1,), token_count, jnp.int32)
    source = source.at[pair_slot.reshape(-1)].set(owners.reshape(-1))
    return (chosen, pair_slot, source[: expert_count * capacity])


def matmul(left, right):
    return jnp.dot(left, right, preferred_element_type=jnp.float32)


def matmul_nt(left, right):
    return lax.dot_general(
        left, right, (((1,), (1,)), ((), ())), preferred_element_type=jnp.float32
    )


def matmul_tn(left, right):
    return lax.dot_general(
        left, right, (((0,), (0,)), ((), ())), preferred_element_type=jnp.float32
    )


def per_device(
    tokens,
    segment_ids,
    routes,
    norm1_gain,
    norm2_gain,
    query_weight,
    key_matrix,
    value_matrix,
    out_weight,
    router_weight,
    gate_weight,
    up_weight,
    down_weight,
    out_grad,
):
    token_count, model_width = tokens.shape
    hid_count = lax.axis_size("hid")
    hid_index = lax.axis_index("hid")
    exp_count = lax.axis_size("exp")
    quarter = model_width // hid_count
    expert_count = router_weight.shape[1]
    local_experts = gate_weight.shape[0]
    topk_count = routes.shape[1]
    capacity = token_count * topk_count * 5 // (4 * expert_count)
    head_size = HEAD_DIM
    block = min(512, token_count)
    block_count = token_count // block
    scale_score = head_size ** (-0.5)
    gain_one, gain_two, w_query, key_projection_weight, value_projection_weight, w_out, w_router = (
        lax.all_gather(norm1_gain.astype(jnp.bfloat16), "exp", axis=0, tiled=True),
        lax.all_gather(norm2_gain.astype(jnp.bfloat16), "exp", axis=0, tiled=True),
        lax.all_gather(query_weight.astype(jnp.bfloat16), "exp", axis=0, tiled=True),
        lax.all_gather(key_matrix.astype(jnp.bfloat16), "exp", axis=0, tiled=True),
        lax.all_gather(value_matrix.astype(jnp.bfloat16), "exp", axis=0, tiled=True),
        lax.all_gather(out_weight.astype(jnp.bfloat16), "exp", axis=0, tiled=True),
        lax.all_gather(router_weight.astype(jnp.bfloat16), "exp", axis=0, tiled=True),
    )
    gain_one = gain_one.astype(jnp.float32)
    gain_two = gain_two.astype(jnp.float32)
    query_heads = w_query.shape[1] // head_size
    kv_heads = key_projection_weight.shape[1] // head_size
    group_size = query_heads // kv_heads
    segments = segment_ids[0]
    positions = positions_of(segments, SEGS)
    cosine, sine = rope_tables(positions, head_size)
    inputs = tokens.astype(jnp.float32)
    scale_one = rms_scale(inputs)
    normed_one = (inputs * scale_one * gain_one[None, :]).astype(jnp.bfloat16)
    query_rows = rotate(
        matmul(normed_one, w_query).reshape(token_count, query_heads, head_size), cosine, sine
    ).astype(jnp.bfloat16)
    key_rows = rotate(
        matmul(normed_one, key_projection_weight).reshape(token_count, kv_heads, head_size),
        cosine,
        sine,
    ).astype(jnp.bfloat16)
    value_rows = (
        matmul(normed_one, value_projection_weight)
        .reshape(token_count, kv_heads, head_size)
        .astype(jnp.bfloat16)
    )
    query_blocks = query_rows.reshape(block_count, block, kv_heads, group_size, head_size)
    starts = jnp.arange(block_count, dtype=jnp.int32) * block
    columns = jnp.arange(token_count, dtype=jnp.int32)

    def block_scores(query_block, start):
        raw_scores = (
            jnp.einsum("qkgd,skd->kgqs", query_block, key_rows, preferred_element_type=jnp.float32)
            * scale_score
        )
        row_ids = start + jnp.arange(block, dtype=jnp.int32)
        row_segments = lax.dynamic_slice_in_dim(segments, start, block)
        allowed = (row_segments[:, None] == segments[None, :]) & (
            row_ids[:, None] >= columns[None, :]
        )
        return jnp.where(allowed[None, None], raw_scores, NEG_FILL)

    def forward_block(packed):
        query_block, start = packed
        scores = block_scores(query_block, start)
        peak = jnp.max(scores, axis=-1, keepdims=True)
        powers = jnp.exp(scores - peak)
        row_total = jnp.sum(powers, axis=-1, keepdims=True)
        probs = (powers / row_total).astype(jnp.bfloat16)
        mixed_block = jnp.einsum(
            "kgqs,skd->qkgd", probs, value_rows, preferred_element_type=jnp.float32
        )
        return (mixed_block, (peak + jnp.log(row_total))[..., 0])

    mixed_blocks, lse_blocks = lax.map(forward_block, (query_blocks, starts))
    mixed = mixed_blocks.reshape(token_count, query_heads * head_size).astype(jnp.bfloat16)
    attn = lax.psum(matmul_nt(mixed, w_out), "hid")
    resid = inputs + attn
    scale_two = rms_scale(resid)
    normed_two = (resid * scale_two * gain_two[None, :]).astype(jnp.bfloat16)
    logits = matmul(normed_two, w_router)
    chosen, pair_slot, source = slot_tables(routes, expert_count, capacity)
    chosen_f = chosen.astype(jnp.float32)
    picked = jnp.sum(chosen_f * logits[:, None, :], axis=2)
    peak_gate = jnp.max(picked, axis=1, keepdims=True)
    gate_powers = jnp.exp(picked - peak_gate)
    gates = gate_powers / jnp.sum(gate_powers, axis=1, keepdims=True)
    padded = jnp.concatenate([normed_two, jnp.zeros((1, model_width), jnp.bfloat16)], axis=0)
    outgoing = padded[source].reshape(expert_count, capacity, model_width)
    gate_b = gate_weight.astype(jnp.bfloat16)
    up_b = up_weight.astype(jnp.bfloat16)
    down_t = jnp.swapaxes(down_weight.astype(jnp.bfloat16), 1, 2)
    arrived = lax.all_to_all(outgoing, "exp", split_axis=0, concat_axis=0, tiled=True)
    slot_rows = arrived.reshape(exp_count, local_experts, capacity, model_width)
    gate_use, up_use, down_use = (gate_b, up_b, down_t)
    gate_pre = jnp.einsum("secd,edf->secf", slot_rows, gate_use, preferred_element_type=jnp.float32)
    up_pre = jnp.einsum("secd,edf->secf", slot_rows, up_use, preferred_element_type=jnp.float32)
    sigmoid_gate = jax.nn.sigmoid(gate_pre)
    silu_gate = gate_pre * sigmoid_gate
    hidden = (silu_gate * up_pre).astype(jnp.bfloat16)
    partial_out = jnp.einsum("secf,edf->secd", hidden, down_use, preferred_element_type=jnp.float32)
    expert_rows = lax.psum_scatter(partial_out, "hid", scatter_dimension=3, tiled=True).astype(
        jnp.bfloat16
    )
    returned = lax.all_to_all(
        expert_rows.reshape(expert_count, capacity, quarter),
        "exp",
        split_axis=0,
        concat_axis=0,
        tiled=True,
    )
    flat_out = jnp.concatenate(
        [returned.reshape(expert_count * capacity, quarter), jnp.zeros((1, quarter), jnp.bfloat16)],
        axis=0,
    )
    paired = flat_out[pair_slot]
    combined = jnp.sum(gates[:, :, None] * paired.astype(jnp.float32), axis=1)
    resid_part = lax.dynamic_slice_in_dim(resid, hid_index * quarter, quarter, 1)
    layer_out = (resid_part + combined).astype(jnp.bfloat16)
    grad_part = out_grad.astype(jnp.float32)
    gate_grad_part = jnp.sum(grad_part[:, None, :] * paired.astype(jnp.float32), axis=2)
    slot_gate = (
        jnp.zeros((expert_count * capacity + 1,), jnp.float32)
        .at[pair_slot.reshape(-1)]
        .set(gates.reshape(-1))[: expert_count * capacity]
    )
    grad_padded = jnp.concatenate([out_grad, jnp.zeros((1, quarter), jnp.bfloat16)], axis=0)
    slot_grad = (slot_gate[:, None] * grad_padded[source].astype(jnp.float32)).astype(jnp.bfloat16)
    grad_arrived = lax.all_to_all(
        slot_grad.reshape(expert_count, capacity, quarter),
        "exp",
        split_axis=0,
        concat_axis=0,
        tiled=True,
    )
    grad_arrived = grad_arrived.reshape(exp_count, local_experts, capacity, quarter)
    grad_rows = lax.all_gather(grad_arrived, "hid", axis=3, tiled=True)
    hidden_grad = jnp.einsum(
        "secd,edf->secf", grad_rows, down_use, preferred_element_type=jnp.float32
    )
    down_grad_t = jnp.einsum(
        "secd,secf->edf", grad_rows, hidden, preferred_element_type=jnp.float32
    )
    pre_gate_grad = (
        hidden_grad * up_pre * sigmoid_gate * (1.0 + gate_pre * (1.0 - sigmoid_gate))
    ).astype(jnp.bfloat16)
    pre_up_grad = (hidden_grad * silu_gate).astype(jnp.bfloat16)
    gate_grad_w = jnp.einsum(
        "secd,secf->edf", slot_rows, pre_gate_grad, preferred_element_type=jnp.float32
    )
    up_grad_w = jnp.einsum(
        "secd,secf->edf", slot_rows, pre_up_grad, preferred_element_type=jnp.float32
    )
    slot_input = jnp.einsum(
        "secf,edf->secd", pre_gate_grad, gate_use, preferred_element_type=jnp.float32
    )
    slot_input = slot_input + jnp.einsum(
        "secf,edf->secd", pre_up_grad, up_use, preferred_element_type=jnp.float32
    )
    slot_share = lax.psum_scatter(slot_input, "hid", scatter_dimension=3, tiled=True).astype(
        jnp.bfloat16
    )
    down_grad = jnp.swapaxes(down_grad_t, 1, 2)
    back_rows = lax.all_to_all(
        slot_share.reshape(expert_count, capacity, quarter),
        "exp",
        split_axis=0,
        concat_axis=0,
        tiled=True,
    )
    flat_back = jnp.concatenate(
        [
            back_rows.reshape(expert_count * capacity, quarter),
            jnp.zeros((1, quarter), jnp.bfloat16),
        ],
        axis=0,
    )
    normed_grad_part = jnp.sum(flat_back[pair_slot].astype(jnp.float32), axis=1)
    grad_full, normed_grad_moe, gate_grad_all = (
        lax.all_gather(grad_part, "hid", axis=1, tiled=True),
        lax.all_gather(normed_grad_part, "hid", axis=1, tiled=True),
        lax.all_gather(gate_grad_part, "hid", axis=1, tiled=True),
    )
    gate_grad = jnp.sum(gate_grad_all.reshape(token_count, hid_count, topk_count), axis=1)
    picked_grad = gates * (gate_grad - jnp.sum(gates * gate_grad, axis=1, keepdims=True))
    logit_grad = jnp.sum(chosen_f * picked_grad[:, :, None], axis=1).astype(jnp.bfloat16)
    normed_grad = normed_grad_moe + matmul_nt(logit_grad, w_router)
    router_grad = matmul_tn(normed_two, logit_grad)
    gain_two_grad = jnp.sum(normed_grad * resid * scale_two, axis=0)
    resid_grad = grad_full + norm_back(normed_grad, resid, scale_two, gain_two)
    resid_grad_b = resid_grad.astype(jnp.bfloat16)
    mixed_grad = matmul(resid_grad_b, w_out).astype(jnp.bfloat16)
    out_grad_w = matmul_tn(resid_grad_b, mixed)
    grad_blocks = mixed_grad.reshape(block_count, block, kv_heads, group_size, head_size)

    def backward_block(carry, packed):
        key_acc, value_acc = carry
        query_block, grad_block, lse_block, start = packed
        scores = block_scores(query_block, start)
        probs = jnp.exp(scores - lse_block[..., None])
        prob_grad = jnp.einsum(
            "qkgd,skd->kgqs", grad_block, value_rows, preferred_element_type=jnp.float32
        )
        inner = jnp.sum(probs * prob_grad, axis=-1, keepdims=True)
        score_grad = (probs * (prob_grad - inner)).astype(jnp.bfloat16)
        query_part = (
            jnp.einsum("kgqs,skd->qkgd", score_grad, key_rows, preferred_element_type=jnp.float32)
            * scale_score
        )
        key_acc = (
            key_acc
            + jnp.einsum(
                "kgqs,qkgd->skd", score_grad, query_block, preferred_element_type=jnp.float32
            )
            * scale_score
        )
        value_acc = value_acc + jnp.einsum(
            "kgqs,qkgd->skd",
            probs.astype(jnp.bfloat16),
            grad_block,
            preferred_element_type=jnp.float32,
        )
        return ((key_acc, value_acc), query_part)

    zero_heads = jnp.zeros((token_count, kv_heads, head_size), jnp.float32)
    (key_sum, value_sum), query_parts = lax.scan(
        backward_block, (zero_heads, zero_heads), (query_blocks, grad_blocks, lse_blocks, starts)
    )
    query_grad = (
        rotate_back(query_parts.reshape(token_count, query_heads, head_size), cosine, sine)
        .reshape(token_count, query_heads * head_size)
        .astype(jnp.bfloat16)
    )
    key_grad = (
        rotate_back(key_sum, cosine, sine)
        .reshape(token_count, kv_heads * head_size)
        .astype(jnp.bfloat16)
    )
    value_grad = value_sum.reshape(token_count, kv_heads * head_size).astype(jnp.bfloat16)
    query_grad_w = matmul_tn(normed_one, query_grad)
    key_grad_w = matmul_tn(normed_one, key_grad)
    value_grad_w = matmul_tn(normed_one, value_grad)
    normed_one_part = (
        matmul_nt(query_grad, w_query)
        + matmul_nt(key_grad, key_projection_weight)
        + matmul_nt(value_grad, value_projection_weight)
    )
    normed_one_grad = lax.psum(normed_one_part.astype(jnp.bfloat16), "hid").astype(jnp.float32)
    gain_one_grad = jnp.sum(normed_one_grad * inputs * scale_one, axis=0)
    input_grad = resid_grad + norm_back(normed_one_grad, inputs, scale_one, gain_one)
    summed_grads = (
        lax.psum_scatter(
            gain_one_grad.astype(jnp.bfloat16), "exp", scatter_dimension=0, tiled=True
        ).astype(jnp.float32),
        lax.psum_scatter(
            gain_two_grad.astype(jnp.bfloat16), "exp", scatter_dimension=0, tiled=True
        ).astype(jnp.float32),
        lax.psum_scatter(
            query_grad_w.astype(jnp.bfloat16), "exp", scatter_dimension=0, tiled=True
        ).astype(jnp.float32),
        lax.psum_scatter(
            key_grad_w.astype(jnp.bfloat16), "exp", scatter_dimension=0, tiled=True
        ).astype(jnp.float32),
        lax.psum_scatter(
            value_grad_w.astype(jnp.bfloat16), "exp", scatter_dimension=0, tiled=True
        ).astype(jnp.float32),
        lax.psum_scatter(
            out_grad_w.astype(jnp.bfloat16), "exp", scatter_dimension=0, tiled=True
        ).astype(jnp.float32),
        lax.psum_scatter(
            router_grad.astype(jnp.bfloat16), "exp", scatter_dimension=0, tiled=True
        ).astype(jnp.float32),
    )
    return (
        layer_out,
        input_grad,
        summed_grads[0],
        summed_grads[1],
        summed_grads[2],
        summed_grads[3],
        summed_grads[4],
        summed_grads[5],
        summed_grads[6],
        gate_grad_w,
        up_grad_w,
        down_grad,
    )


def solution(mesh):
    in_specs = (
        P("exp", None),
        P("exp", None),
        P("exp", None),
        P("exp"),
        P("exp"),
        P("exp", "hid"),
        P("exp", "hid"),
        P("exp", "hid"),
        P("exp", "hid"),
        P("exp", None),
        P("exp", None, "hid"),
        P("exp", None, "hid"),
        P("exp", "hid", None),
        P("exp", "hid"),
    )
    out_specs = (
        P("exp", "hid"),
        P("exp", None),
        P("exp"),
        P("exp"),
        P("exp", "hid"),
        P("exp", "hid"),
        P("exp", "hid"),
        P("exp", "hid"),
        P("exp", None),
        P("exp", None, "hid"),
        P("exp", None, "hid"),
        P("exp", "hid", None),
    )
    return jax.shard_map(
        per_device, mesh=mesh, in_specs=in_specs, out_specs=out_specs, check_vma=False
    )
```

profile of v0, /device:TPU:0, one launch (start us, length us, event | category | flops | bytes accessed | tf_op | source)
XLA Modules:
  0.0 2167.6 jit_solution(6931939964201163253)
XLA Ops:
  9.1 22.1 %all-gather = bf16[8,1,128]{2,1,0:T(2,128)(2,1)S(1)} all-gather(bf16[1,1,128]{2,1,0:T(2,128)(2,1)S(1)} %convert_bitcast_fusion.1), channel_id=1, replica_groups=mesh['exp'=8,'hid'=4] {'exp'}, dimensions={0}, use_global_device_ids=true | all-gather | bytes 2304 | tf_op jit(solution)/shard_map/all_gather | solution.py:119
  38.2 30.7 %all_gather.36 = bf16[1024,128]{1,0:T(8,128)(2,1)S(1)} all-gather(bf16[128,128]{1,0:T(8,128)(2,1)S(1)} %convert_element_type.201), channel_id=1, replica_groups=mesh['exp'=8,'hid'=4] {'exp'}, dimensions={0}, use_global_device_ids=true | all-gather | bytes 294912 | tf_op jit(solution)/shard_map/all_gather | solution.py:123
  68.9 30.7 %all_gather.35 = bf16[1024,128]{1,0:T(8,128)(2,1)S(1)} all-gather(bf16[128,128]{1,0:T(8,128)(2,1)S(1)} %convert_element_type.200), channel_id=1, replica_groups=mesh['exp'=8,'hid'=4] {'exp'}, dimensions={0}, use_global_device_ids=true | all-gather | bytes 294912 | tf_op jit(solution)/shard_map/all_gather | solution.py:122
  99.6 31.5 %all_gather.37 = bf16[1024,256]{1,0:T(8,128)(2,1)S(1)} all-gather(bf16[128,256]{1,0:T(8,128)(2,1)S(1)} %convert_element_type.206), channel_id=1, replica_groups=mesh['exp'=8,'hid'=4] {'exp'}, dimensions={0}, use_global_device_ids=true | all-gather | bytes 589824 | tf_op jit(solution)/shard_map/all_gather | solution.py:124
  131.2 31.2 %all_gather.34 = bf16[1024,256]{1,0:T(8,128)(2,1)S(1)} all-gather(bf16[128,256]{1,0:T(8,128)(2,1)S(1)} %convert_element_type.197), channel_id=1, replica_groups=mesh['exp'=8,'hid'=4] {'exp'}, dimensions={0}, use_global_device_ids=true | all-gather | bytes 589824 | tf_op jit(solution)/shard_map/all_gather | solution.py:121
  170.4 27.7 %while.28 = (s32[]{:T(128)}, bf16[2,512,2,2,64]{1,4,3,2,0:T(8,128)(2,1)}, f32[2,2,2,512]{3,2,1,0:T(2,128)}, s32[2]{0:T(128)S(1)}, s32[1024]{0:T(1024)S(1)}, /*in...) while((s32[]{:T(128)}, ...), condition=%wide.region_7.8_spmd.clone, body=%wide.region_4.7_spmd.clone.sunk | while | flops 563608064 | bytes 32979248 | solution.py:179
  203.7 16.8 all-gather.1
  220.6 9.0 reduce-window.19
  231.8 30.5 %scatter_custom_fusion = s32[10241]{0:T(1024)S(1)} fusion(s32[8192]{0:T(1024)S(1)} %bitcast.388, s32[8192]{0:T(1024)S(1)} %reshape.554, s32[]{:T(128)} %constant.58.clone.1), kind=kCustom, calls=%fused_computation.190 | custom fusion | bytes 40968 | tf_op jit(solution)/shard_map/scatter | solution.py:69
  262.3 41.1 %gather_fusion.2 = bf16[10240,256]{1,0:T(8,128)(2,1)} fusion(bf16[1025,256]{1,0:T(8,128)(2,1)S(1)} %concatenate.39, s32[10240]{0:T(1024)S(1)} %fusion.109), kind=kCustom, calls=%fused_computation.2 | custom fusion | bytes 10526720 | tf_op jit(solution)/shard_map/gather | solution.py:232
  303.5 26.0 %all_gather.39 = bf16[1024,32]{0,1:T(8,128)(2,1)S(1)} all-gather(bf16[128,32]{0,1:T(8,128)(2,1)S(1)} %convert_element_type.210), channel_id=1, replica_groups=mesh['exp'=8,'hid'=4] {'exp'}, dimensions={0}, use_global_device_ids=true | all-gather | bytes 73728 | tf_op jit(solution)/shard_map/all_gather | solution.py:125
  338.3 30.5 %scatter_custom_fusion.1 = f32[10241]{0:T(1024)S(1)} fusion(s32[8192]{0:T(1024)S(1)} %bitcast.389, f32[8192]{0:T(1024)S(1)} %reshape.562, f32[]{:T(128)} %constant.36.clone.1), kind=kCustom, calls=%fused_computation.188 | custom fusion | bytes 40968 | tf_op jit(solution)/shard_map/scatter | solution.py:229
  368.9 6.6 fusion.60
  381.9 44.1 %gather_fusion = bf16[10240,1024]{1,0:T(8,128)(2,1)} fusion(bf16[1025,1024]{1,0:T(8,128)(2,1)S(1)} %concatenate.37, s32[10240]{0:T(1024)S(1)} %fusion.109), kind=kCustom, calls=%fused_computation | custom fusion | bytes 41984000 | tf_op jit(solution)/shard_map/gather | solution.py:193
  425.9 40.0 %all-to-all-done.2 = bf16[32,320,256]{2,1,0:T(8,128)(2,1)} async-done(((bf16[32,320,256]{2,1,0:T(8,128)(2,1)}), bf16[32,320,256]{2,1,0:T(8,128)(2,1)}, u32[]{:S(2)}, u32[]{:S(2)}) %all-to-all-start.2) | async-done | bytes 5242912 | tf_op jit(solution)/shard_map/all_to_all | solution.py:233
  465.9 59.5 %all-to-all-start = ((bf16[32,320,1024]{2,1,0:T(8,128)(2,1)}), bf16[32,320,1024]{2,1,0:T(8,128)(2,1)}, u32[]{:S(2)}, u32[]{:S(2)}) async-start(bf16[32,320,1024]{2,1,0:T(8,128)(2,1)} %bitcast.354), calls=%async_computation | async-start | bytes 41943040 | tf_op jit(solution)/shard_map/all_to_all | solution.py:197
  525.5 5.4 copy.109
  531.1 379.3 %all-to-all-done = bf16[32,320,1024]{2,1,0:T(8,128)(2,1)} async-done(((bf16[32,320,1024]{2,1,0:T(8,128)(2,1)}), bf16[32,320,1024]{2,1,0:T(8,128)(2,1)}, u32[]{:S(2)}, u32[]{:S(2)}) %all-to-all-start) | async-done | bytes 20971552 | tf_op jit(solution)/shard_map/all_to_all | solution.py:197
  910.5 11.6 fusion.56
  922.1 11.4 fusion.58
  933.5 15.6 fusion.66
  949.1 16.4 fusion.94
  965.6 28.3 %add_bitcast_fusion = f32[8,4,320,1024]{3,2,0,1:T(8,128)} fusion(f32[4,8,320,1024]{3,2,1,0:T(8,128)} %fusion.94, bf16[8,4,320,128]{3,2,0,1:T(8,128)(2,1)} %get-tuple-element.354, f32[4,1024,128]{2,1,0:T(8,128)} %param.29), kind=kOutput, calls=%fused_computation.70 | convolution fusion | flops 2695364608 | bytes 88604672 | tf_op jit(solution)/shard_map/secf,edf->secd/dot_general | solution.py:261
  993.9 28.1 %convolution_bitcast_fusion.1 = f32[8,4,320,1024]{3,2,0,1:T(8,128)} fusion(bf16[8,4,320,128]{3,2,0,1:T(8,128)(2,1)S(1)} %get-tuple-element.356, f32[4,128,1024]{2,1,0:T(8,128)} %param.30), kind=kOutput, calls=%fused_computation.75 | convolution fusion | flops 2684878848 | bytes 46661632 | tf_op jit(solution)/shard_map/secf,edf->secd/dot_general | solution.py:205
  1022.0 259.1 %reduce-scatter.12.cloned.1.call-done = f32[8,4,320,256]{3,2,0,1:T(8,128)} async-done(((f32[8,4,320,1024]{3,2,0,1:T(8,128)}), f32[8,4,320,256]{3,2,0,1:T(8,128)}) %reduce-scatter.12.cloned.1.call-update) | async-done | bytes 10485776 | tf_op jit(solution)/shard_map/reduce_scatter | solution.py:264
  1288.5 5.6 all-to-all-start.3
  1294.7 115.2 %all-to-all-done.3 = bf16[32,320,256]{2,1,0:T(8,128)(2,1)} async-done(((bf16[32,320,256]{2,1,0:T(8,128)(2,1)}), bf16[32,320,256]{2,1,0:T(8,128)(2,1)}, u32[]{:S(2)}, u32[]{:S(2)}) %all-to-all-start.3) | async-done | bytes 5242912 | tf_op jit(solution)/shard_map/all_to_all | solution.py:268
  1414.9 34.3 %gather_fusion.3 = bf16[8192,256]{1,0:T(8,128)(2,1)} fusion(bf16[10241,256]{1,0:T(8,128)(2,1)} %concatenate.40, s32[8192]{0:T(1024)S(1)} %broadcast_clamp_fusion), kind=kCustom, calls=%fused_computation.3 | custom fusion | bytes 8421376 | tf_op jit(solution)/shard_map/gather | solution.py:282
  1449.2 5.9 convert_reduce_fusion
  1455.1 117.2 %reduce-scatter.10.cloned.1.call-done = f32[8,4,320,256]{3,2,0,1:T(8,128)} async-done(((f32[8,4,320,1024]{3,2,0,1:T(8,128)}), f32[8,4,320,256]{3,2,0,1:T(8,128)}) %reduce-scatter.10.cloned.1.call-update) | async-done | bytes 10485776 | tf_op jit(solution)/shard_map/reduce_scatter | solution.py:206
  1579.7 5.6 all-to-all-start.1
  1587.8 113.3 %all-to-all-done.1 = bf16[32,320,256]{2,1,0:T(8,128)(2,1)} async-done(((bf16[32,320,256]{2,1,0:T(8,128)(2,1)}), bf16[32,320,256]{2,1,0:T(8,128)(2,1)}, u32[]{:S(2)}, u32[]{:S(2)}) %all-to-all-start.1) | async-done | bytes 5242912 | tf_op jit(solution)/shard_map/all_to_all | solution.py:209
  1705.4 34.4 %gather_fusion.1 = bf16[8192,256]{1,0:T(8,128)(2,1)} fusion(bf16[10241,256]{1,0:T(8,128)(2,1)} %concatenate.38, s32[8192]{0:T(1024)S(1)} %broadcast_clamp_fusion), kind=kCustom, calls=%fused_computation.1 | custom fusion | bytes 8421376 | tf_op jit(solution)/shard_map/gather | solution.py:220
  1739.8 14.4 fusion.62
  1755.4 5.4 all_gather.43
  1762.5 7.3 multiply_reduce_fusion
  1769.8 5.5 subtract_add_fusion
  1780.8 64.2 %while.29 = (s32[]{:T(128)}, f32[1024,2,64]{0,2,1:T(8,128)S(1)}, f32[1024,2,64]{0,2,1:T(8,128)}, f32[2,512,2,2,64]{1,0,4,3,2:T(2,128)}, bf16[2,512,2,2,64]{1,4,3...) while((s32[]{:T(128)}, f32[1024,2,64]{0,2,1:T(8,128)S(1)}, ...), condition=%wide.region_30.31_spmd.clone, body=%wide.region_28.30_spmd.clone.sunk | while | flops 1375992320 | bytes 71637232 | solution.py:330
  1802.5 10.4 dynamic_update_slice.21
  1834.6 10.4 dynamic_update_slice.21
  1847.6 13.1 fusion.89
  1878.4 13.2 fusion.86
  1893.3 12.3 convolution_bitcast_fusion.2
  1910.7 60.4 %reduce-scatter.18.cloned.1.call-done = bf16[128,128]{1,0:T(8,128)(2,1)} async-done(((bf16[1024,128]{1,0:T(8,128)(2,1)}), bf16[128,128]{1,0:T(8,128)(2,1)}) %reduce-scatter.18.cloned.1.call-update) | async-done | bytes 32784 | tf_op jit(solution)/shard_map/reduce_scatter | solution.py:368
  1972.5 63.2 %reduce-scatter.20.cloned.1.call-done = bf16[128,256]{1,0:T(8,128)(2,1)} async-done(((bf16[1024,256]{1,0:T(8,128)(2,1)}), bf16[128,256]{1,0:T(8,128)(2,1)}) %reduce-scatter.20.cloned.1.call-update) | async-done | bytes 65552 | tf_op jit(solution)/shard_map/reduce_scatter | solution.py:371
  2037.2 51.3 %all-reduce.12.cloned.1.call-done = bf16[1024,1024]{1,0:T(8,128)(2,1)} async-done(((bf16[1024,1024]{1,0:T(8,128)(2,1)}), bf16[1024,1024]{1,0:T(8,128)(2,1)}) %all-reduce.12.cloned.1.call-update) | async-done | bytes 2097168 | tf_op jit(solution)/shard_map/psum | solution.py:352
  2091.7 21.4 all-reduce.6
  2113.7 40.3 %reduce-scatter.14.cloned.1.call-done = bf16[128,256]{1,0:T(8,128)(2,1)} async-done(((bf16[1024,256]{1,0:T(8,128)(2,1)}), bf16[128,256]{1,0:T(8,128)(2,1)}) %reduce-scatter.14.cloned.1.call-update) | async-done | bytes 65552 | tf_op jit(solution)/shard_map/reduce_scatter | solution.py:362
  (338 shorter events, 177.6 us)
Async XLA Ops:
  7.2 155.1 %copy-start.5 = (bf16[1024,1024]{1,0:T(8,128)(2,1)S(1)}, bf16[1024,1024]{1,0:T(8,128)(2,1)}, u32[]{:S(2)}) copy-start(bf16[1024,1024]{1,0:T(8,128)(2,1)} %param.18) | copy-start | bytes 6291460
  7.2 322.3 %all-reduce.10.cloned.1.call-start = ((), (), s32[]{:S(2)}) async-start(), calls=%async_computation.11 | async-start | bytes 8388608 | tf_op jit(solution)/shard_map/psum | solution.py:181
  31.2 131.7 %copy-start.62 = (f32[8,1,128]{2,1,0:T(1,128)}, f32[8,1,128]{2,1,0:T(1,128)S(1)}, u32[]{:S(2)}) copy-start(f32[8,1,128]{2,1,0:T(1,128)S(1)} %convert_element_type.253) | copy-start | bytes 12292
  34.6 129.8 %copy-start.60 = (f32[1024]{0:T(1024)}, f32[1024]{0:T(1024)S(1)}, u32[]{:S(2)}) copy-start(f32[1024]{0:T(1024)S(1)} %get-tuple-element.368) | copy-start | bytes 12292
  68.9 96.4 %copy-start.28 = (bf16[1024,128]{1,0:T(8,128)(2,1)}, bf16[1024,128]{1,0:T(8,128)(2,1)S(1)}, u32[]{:S(2)}) copy-start(bf16[1024,128]{1,0:T(8,128)(2,1)S(1)} %all_gather.36) | copy-start | bytes 786436
  99.6 65.7 %copy-start.30 = (bf16[1024,128]{1,0:T(8,128)(2,1)}, bf16[1024,128]{1,0:T(8,128)(2,1)S(1)}, u32[]{:S(2)}) copy-start(bf16[1024,128]{1,0:T(8,128)(2,1)S(1)} %all_gather.35) | copy-start | bytes 786436
  131.1 68.8 %copy-start.18 = (bf16[1024,256]{1,0:T(8,128)(2,1)}, bf16[1024,256]{1,0:T(8,128)(2,1)S(1)}, u32[]{:S(2)}) copy-start(bf16[1024,256]{1,0:T(8,128)(2,1)S(1)} %all_gather.37) | copy-start | bytes 1572868
  200.8 19.7 copy-start.66
  200.8 19.7 copy-start.43
  203.6 58.7 %copy-start.37 = (bf16[1024,256]{1,0:T(8,128)(2,1)S(1)}, bf16[1024,256]{1,0:T(8,128)(2,1)}, u32[]{:S(2)}) copy-start(bf16[1024,256]{1,0:T(8,128)(2,1)} %param.31) | copy-start | bytes 1572868
  220.5 112.5 %copy-start.56 = (f32[8,1,128]{2,1,0:T(1,128)}, f32[8,1,128]{2,1,0:T(1,128)S(1)}, u32[]{:S(2)}) copy-start(f32[8,1,128]{2,1,0:T(1,128)S(1)} %convert_element_type.254) | copy-start | bytes 12292
  338.1 37.4 %copy-start.12 = (f32[1024,8]{1,0:T(8,128)}, f32[1024,8]{1,0:T(8,128)S(1)}, u32[]{:S(2)}) copy-start(f32[1024,8]{1,0:T(8,128)S(1)} %copy.100) | copy-start | bytes 98308
  375.5 90.5 %all-to-all-start.2 = ((bf16[32,320,256]{2,1,0:T(8,128)(2,1)}), bf16[32,320,256]{2,1,0:T(8,128)(2,1)}, u32[]{:S(2)}, u32[]{:S(2)}) async-start(bf16[32,320,256]{2,1,0:T(8,128)(2,1)} %fusion.60), calls=%async_computation.3 | async-start | bytes 10485760 | tf_op jit(solution)/shard_map/all_to_all | solution.py:233
  465.9 444.5 %all-to-all-start = ((bf16[32,320,1024]{2,1,0:T(8,128)(2,1)}), bf16[32,320,1024]{2,1,0:T(8,128)(2,1)}, u32[]{:S(2)}, u32[]{:S(2)}) async-start(bf16[32,320,1024]{2,1,0:T(8,128)(2,1)} %bitcast.354), calls=%async_computation | async-start | bytes 41943040 | tf_op jit(solution)/shard_map/all_to_all | solution.py:197
  525.5 408.0 %all-gather.8.cloned.1.call-start = ((), (), s32[]{:S(2)}) async-start(), calls=%async_computation.14 | async-start | bytes 26214400 | tf_op jit(solution)/shard_map/all_gather | solution.py:241
  530.9 379.6 %copy-start.34 = (f32[4,1024,128]{2,1,0:T(8,128)S(1)}, f32[4,1024,128]{2,1,0:T(8,128)}, u32[]{:S(2)}) copy-start(f32[4,1024,128]{2,1,0:T(8,128)} %param.29) | copy-start | bytes 6291460
  530.9 750.2 %reduce-scatter.12.cloned.1.call-start = ((), (), s32[]{:S(2)}) async-start(), calls=%async_computation.15 | async-start | bytes 52428800 | tf_op jit(solution)/shard_map/reduce_scatter | solution.py:264
  933.5 15.6 copy-start.33
  949.1 16.5 copy-start.25
  949.1 44.8 %copy-start.4 = (bf16[8,4,320,128]{3,2,0,1:T(8,128)(2,1)}, bf16[8,4,320,128]{3,2,0,1:T(8,128)(2,1)S(1)}, u32[]{:S(2)}) copy-start(bf16[8,4,320,128]{3,2,0,1:T(8,128)(2,1)S(1)} %get-tuple-element.356) | copy-start | bytes 7864324
  993.9 578.5 %reduce-scatter.10.cloned.1.call-start = ((), (), s32[]{:S(2)}) async-start(), calls=%async_computation.12 | async-start | bytes 52428800 | tf_op jit(solution)/shard_map/reduce_scatter | solution.py:206
  1288.5 121.4 %all-to-all-start.3 = ((bf16[32,320,256]{2,1,0:T(8,128)(2,1)}), bf16[32,320,256]{2,1,0:T(8,128)(2,1)}, u32[]{:S(2)}, u32[]{:S(2)}) async-start(bf16[32,320,256]{2,1,0:T(8,128)(2,1)} %bitcast.356), calls=%async_computation.5 | async-start | bytes 10485760 | tf_op jit(solution)/shard_map/all_to_all | solution.py:268
  1294.1 468.3 %all-gather.10.cloned.1.call-start = ((), (), s32[]{:S(2)}) async-start(), calls=%async_computation.16 | async-start | bytes 5242880 | tf_op jit(solution)/shard_map/all_gather | solution.py:285
  1579.7 121.4 %all-to-all-start.1 = ((bf16[32,320,256]{2,1,0:T(8,128)(2,1)}), bf16[32,320,256]{2,1,0:T(8,128)(2,1)}, u32[]{:S(2)}, u32[]{:S(2)}) async-start(bf16[32,320,256]{2,1,0:T(8,128)(2,1)} %bitcast.355), calls=%async_computation.2 | async-start | bytes 10485760 | tf_op jit(solution)/shard_map/all_to_all | solution.py:209
  1585.3 184.5 %all-gather.6.cloned.1.call-start = ((), (), s32[]{:S(2)}) async-start(), calls=%async_computation.13 | async-start | bytes 5242880 | tf_op jit(solution)/shard_map/all_gather | solution.py:284
  1586.5 321.4 %reduce-scatter.22.cloned.1.call-start = ((), (), s32[]{:S(2)}) async-start(), calls=%async_computation.22 | async-start | bytes 294912
  1705.4 34.4 %copy-start.13 = (f32[1024,8]{1,0:T(8,128)S(1)}, f32[1024,8]{1,0:T(8,128)}, u32[]{:S(2)}) copy-start(f32[1024,8]{1,0:T(8,128)} %copy-done.12) | copy-start | bytes 98308
  1739.7 21.1 copy-start.42
  1739.7 21.1 copy-start.51
  1739.8 21.1 copy-start.59
  1739.8 21.2 copy-start.44
  1739.8 21.3 copy-start.8
  1739.8 22.7 %copy-start.46 = (bf16[1024,32]{0,1:T(8,128)(2,1)S(1)}, bf16[1024,32]{0,1:T(8,128)(2,1)}, u32[]{:S(2)}) copy-start(bf16[1024,32]{0,1:T(8,128)(2,1)} %copy-done.45) | copy-start | bytes 196612
  1739.8 22.7 %copy-start.55 = (f32[1024]{0:T(1024)S(1)}, f32[1024]{0:T(1024)}, u32[]{:S(2)}) copy-start(f32[1024]{0:T(1024)} %copy-done.54) | copy-start | bytes 12292
  1739.8 22.7 %copy-start.57 = (f32[8,1,128]{2,1,0:T(1,128)S(1)}, f32[8,1,128]{2,1,0:T(1,128)}, u32[]{:S(2)}) copy-start(f32[8,1,128]{2,1,0:T(1,128)} %copy-done.56) | copy-start | bytes 12292
  1762.4 146.9 %reduce-scatter.16.cloned.1.call-start = ((), (), s32[]{:S(2)}) async-start(), calls=%async_computation.19 | async-start | bytes 294912 | tf_op jit(solution)/shard_map/reduce_scatter | solution.py:365
  1780.8 64.2 %copy-start.22 = (f32[1024,32]{0,1:T(8,128)S(1)}, f32[1024,32]{0,1:T(8,128)}, u32[]{:S(2)}) copy-start(f32[1024,32]{0,1:T(8,128)} %copy-done.21) | copy-start | bytes 393220
  1780.8 65.2 %copy-start.1 = (bf16[1024,1024]{1,0:T(8,128)(2,1)S(1)}, bf16[1024,1024]{1,0:T(8,128)(2,1)}, u32[]{:S(2)}) copy-start(bf16[1024,1024]{1,0:T(8,128)(2,1)} %copy-done) | copy-start | bytes 6291460
  1847.5 123.6 %reduce-scatter.18.cloned.1.call-start = ((), (), s32[]{:S(2)}) async-start(), calls=%async_computation.20 | async-start | bytes 294912 | tf_op jit(solution)/shard_map/reduce_scatter | solution.py:368
  1863.3 172.4 %reduce-scatter.20.cloned.1.call-start = ((), (), s32[]{:S(2)}) async-start(), calls=%async_computation.21 | async-start | bytes 589824 | tf_op jit(solution)/shard_map/reduce_scatter | solution.py:371
  1873.0 215.4 %all-reduce.12.cloned.1.call-start = ((), (), s32[]{:S(2)}) async-start(), calls=%async_computation.17 | async-start | bytes 4194304 | tf_op jit(solution)/shard_map/psum | solution.py:352
  1878.4 13.3 copy-start.36
  1878.4 275.7 %reduce-scatter.14.cloned.1.call-start = ((), (), s32[]{:S(2)}) async-start(), calls=%async_computation.18 | async-start | bytes 589824 | tf_op jit(solution)/shard_map/reduce_scatter | solution.py:362
  1893.3 195.2 %copy-start.61 = (f32[1024]{0:T(1024)S(1)}, f32[1024]{0:T(1024)}, u32[]{:S(2)}) copy-start(f32[1024]{0:T(1024)} %copy-done.60) | copy-start | bytes 12292
  1893.3 195.2 %copy-start.63 = (f32[8,1,128]{2,1,0:T(1,128)S(1)}, f32[8,1,128]{2,1,0:T(1,128)}, u32[]{:S(2)}) copy-start(f32[8,1,128]{2,1,0:T(1,128)} %copy-done.62) | copy-start | bytes 12292
  1905.6 182.9 %copy-start.6 = (bf16[1024,1024]{1,0:T(8,128)(2,1)S(1)}, bf16[1024,1024]{1,0:T(8,128)(2,1)}, u32[]{:S(2)}) copy-start(bf16[1024,1024]{1,0:T(8,128)(2,1)} %param.18) | copy-start | bytes 6291460
  1905.6 186.1 %copy-start.67 = (bf16[1024]{0:T(1024)(128)(2,1)S(1)}, bf16[1024]{0:T(1024)(128)(2,1)}, u32[]{:S(2)}) copy-start(bf16[1024]{0:T(1024)(128)(2,1)} %get-tuple-element.296) | copy-start | bytes 6148
  1905.6 250.0 %copy-start.64 = (f32[1024]{0:T(1024)S(1)}, f32[1024]{0:T(1024)}, u32[]{:S(2)}) copy-start(f32[1024]{0:T(1024)} %get-tuple-element.367) | copy-start | bytes 12292
  (44 other events, 161.0 us)
Sparse Core Ops, SparseCore 0:
  203.7 82.7 all-reduce.9
  531.0 135.9 all-gather.7
  994.0 287.0 reduce-scatter.11
  1283.5 288.7 reduce-scatter.9
  1573.8 34.4 all-gather.9
  1610.4 34.4 all-gather.5
  1762.5 59.4 reduce-scatter.21
  1847.6 59.3 reduce-scatter.15
  1910.8 60.3 reduce-scatter.17
  1974.7 60.9 reduce-scatter.19
  2038.1 50.3 all-reduce.11
  2092.0 61.9 reduce-scatter.13
where the time goes:
time: 2180 us; the launch traced here: 2170 us
  waiting for transfers between devices  1240 us (57%)
  local copies, waits for them, and re-layouts  287 us (13%)
  matrix products  220 us (10%)
  blocking collectives  216 us (10%)
  other arithmetic  105 us (5%)
  starting transfers between devices  76.1 us (3%)
    all_to_all x1, waiting for transfers between devices, per_device(): lax.all_to_all(outgoing, 'exp', split_axis=0, concat_axis=0, tiled=True)  379 us
    reduce_scatter x1, waiting for transfers between devices, per_device(): lax.psum_scatter(slot_input, 'hid', scatter_dimension=3, tiled=True)  259 us
    reduce_scatter x1, waiting for transfers between devices, per_device(): lax.psum_scatter(partial_out, 'hid', scatter_dimension=3, tiled=True)  117 us
    all_to_all x1, waiting for transfers between devices, per_device(): lax.all_to_all(slot_share.reshape(expert_count, capacity, quarter), 'exp'...  115 us
    all_to_all x1, waiting for transfers between devices, per_device(): lax.all_to_all(expert_rows.reshape(expert_count, capacity, quarter), 'exp...  113 us
    reduce_scatter x1, waiting for transfers between devices, per_device(): lax.psum_scatter(out_grad_w.astype(jnp.bfloat16), 'exp', scatter_dimensio...  63.2 us
    reduce_scatter x1, waiting for transfers between devices, per_device(): lax.psum_scatter(value_grad_w.astype(jnp.bfloat16), 'exp', scatter_dimens...  60.4 us
    all_to_all x1, starting transfers between devices, per_device(): lax.all_to_all(outgoing, 'exp', split_axis=0, concat_axis=0, tiled=True)  59.5 us
  transfers between devices with their start and end apart: 16, of which 10 were waited for; matrix products, arithmetic and copies ran while one was open for 21% of the time, Pallas kernels for 0%

commit v1 on v0

v1 whole, which is shorter than its diff:
```python
import functools

import jax
import jax.numpy as jnp
from jax import lax
from jax.experimental import pallas as pl
from jax.experimental.pallas import tpu as pltpu
from jax.sharding import PartitionSpec as P

HEAD_DIM = 64
SEGS = 4
EPSILON = 1e-05
ROPE_BASE = 10000.0
NEG_FILL = -1e30
LANES = 128
MESH = pl.DeviceIdType.MESH
F32 = jnp.float32
BF16 = jnp.bfloat16
VMEM_LIMIT = 60 * 2**20
SMALL_VMEM = 30 * 2**20


def nn(a, b):
    return lax.dot_general(a, b, (((1,), (0,)), ((), ())), preferred_element_type=F32)


def nt(a, b):
    return lax.dot_general(a, b, (((1,), (1,)), ((), ())), preferred_element_type=F32)


def tn(a, b):
    return lax.dot_general(a, b, (((0,), (0,)), ((), ())), preferred_element_type=F32)


def tn_exact(a, b):
    return lax.dot_general(
        a, b, (((0,), (0,)), ((), ())), preferred_element_type=F32, precision=lax.Precision.HIGHEST
    )


def iota(shape, dim):
    return lax.broadcasted_iota(jnp.int32, shape, dim)


def rows_at(index, size):
    return pl.ds(pl.multiple_of(index * size, size), size)


def pos_of(index, n):
    odd = index % 2
    return (1 - odd) * (index // 2) + odd * (n - 1 - index // 2)


def at_pos(pos, n):
    back = pos // (n // 2)
    return (1 - back) * (2 * pos) + back * (2 * (n - 1 - pos) + 1)


class Place:
    def __init__(self, n):
        self.n = n
        self.e = lax.axis_index("exp")
        self.h = lax.axis_index("hid")
        self.p = pos_of(self.e, n)
        self.right = self.ring(1)
        self.left = self.ring(-1)
        self.sib = self.h + 1 - 2 * (self.h % 2)
        self.far = (self.h + 2) % 4
        self.diag = (self.sib + 2) % 4

    def ring(self, away):
        return at_pos((self.p + self.n + away) % self.n, self.n)


def greet(exp_peers, hid_peers):
    barrier = pltpu.get_barrier_semaphore()
    for peer in exp_peers:
        pl.semaphore_signal(barrier, inc=1, device_id={"exp": peer}, device_id_type=MESH)
    for peer in hid_peers:
        pl.semaphore_signal(barrier, inc=1, device_id={"hid": peer}, device_id_type=MESH)
    pl.semaphore_wait(barrier, len(exp_peers) + len(hid_peers))


def remote(src, dst, sems, k, axis, to):
    return pltpu.make_async_remote_copy(
        src_ref=src,
        dst_ref=dst,
        send_sem=sems.at[0, k],
        recv_sem=sems.at[1, k],
        device_id={axis: to},
        device_id_type=MESH,
    )


class Sent:
    def __init__(self):
        self.copies = {}
        self.unsent = []

    def start(self, key, copy):
        copy.start()
        self.copies[key] = copy
        self.unsent.append(copy)

    def recv(self, key):
        self.copies[key].wait_recv()

    def done(self):
        for copy in self.unsent:
            copy.wait_send()
        self.unsent = []


class RingGather:
    def __init__(self, place, view, rows, sems):
        self.place, self.view, self.rows, self.sems = place, view, rows, sems
        self.steps = place.n // 2
        self.sent = Sent()

    def start(self, s):
        rows, half = self.rows, self.rows // 2
        last = s == self.steps - 1
        for side, (away, to) in enumerate(((-s, self.place.right), (s, self.place.left))):
            first, size = ((side * half, half) if last else (0, rows))
            block = self.view(self.place.ring(away), first, size)
            self.sent.start((s, side), remote(block, block, self.sems, 2 * s + side, "exp", to))

    def recv(self, s):
        self.sent.recv((s, 0))
        self.sent.recv((s, 1))

    def done(self):
        self.sent.done()


class RingSum:
    def __init__(self, place, send, recv, rows, sems):
        self.place, self.send, self.recv, self.rows, self.sems = place, send, recv, rows, sems
        self.steps = place.n // 2
        self.slots = send.shape[1]
        self.copies = {}

    def owner(self, s, side):
        away = self.steps - s
        return self.place.ring(away if side == 0 else -away)

    def room(self, s):
        for side in (0, 1):
            if s >= self.slots:
                self.copies[(s - self.slots, side)].wait_send()

    def buffer(self, s, side):
        return self.send.at[side, s % self.slots]

    def go(self, s):
        half = self.rows // 2
        for side, to in ((0, self.place.right), (1, self.place.left)):
            src, dst = self.send.at[side, s % self.slots], self.recv.at[side, s]
            if s == 0:
                src, dst = src.at[pl.ds(side * half, half)], dst.at[pl.ds(side * half, half)]
            copy = remote(src, dst, self.sems, 2 * s + side, "exp", to)
            copy.start()
            self.copies[(s, side)] = copy

    def arrived(self, s, side):
        self.copies[(s, side)].wait_recv()

    def add_into(self, s, side, get):
        half = self.rows // 2
        out = self.buffer(s, side)
        if s == 0:
            out[pl.ds(side * half, half)] = get(pl.ds(side * half, half)).astype(out.dtype)
            return
        self.arrived(s - 1, side)
        came = self.recv.at[side, s - 1]
        for k in (0, 1):
            part = pl.ds(k * half, half)
            value = get(part)
            if s > 1 or k == side:
                value = value + came[part].astype(F32)
            out[part] = value.astype(out.dtype)

    def total(self, part):
        return self.recv[0, self.steps - 1, part].astype(F32) + self.recv[1, self.steps - 1, part].astype(F32)

    def arrive_last(self):
        self.arrived(self.steps - 1, 0)
        self.arrived(self.steps - 1, 1)

    def done(self):
        for s in range(max(0, self.steps - self.slots), self.steps):
            for side in (0, 1):
                self.copies[(s, side)].wait_send()


def local_start(src, dst, sem):
    copy = pltpu.make_async_copy(src, dst, sem)
    copy.start()
    return copy


def split_parts(count):
    return (pl.ds(0, count // 2), pl.ds(count // 2, count // 2))


def rms(values):
    return lax.rsqrt(jnp.mean(values * values, axis=-1, keepdims=True) + EPSILON)


def swap_halves(values):
    half = HEAD_DIM // 2
    width = values.shape[1]
    up = pltpu.roll(values, width - half, 1)
    down = pltpu.roll(values, half, 1)
    first = iota(values.shape, 1) % HEAD_DIM < half
    return jnp.where(first, up, down)


def gain_rows(slab, expert_count):
    pick = (iota((16, LANES), 1) == iota((16, LANES), 0) + expert_count).astype(BF16)
    return nt(pick, slab)


def bias_block(begin_row, first_row, key_count):
    shape = (key_count, begin_row.shape[1])
    keys = iota(shape, 0)
    seen = (keys >= begin_row) & (keys <= first_row + iota(shape, 1))
    return jnp.where(seen, 0.0, NEG_FILL)


class Dims:
    def __init__(self, n, token_count, width, expert_count, local_experts, ff, topk, qc, kc):
        self.n, self.tokens, self.d = n, token_count, width
        self.experts, self.local, self.ff, self.topk = expert_count, local_experts, ff, topk
        self.qc, self.kc = qc, kc
        self.quarter = token_count // 4
        self.shard = width // n
        self.capacity = token_count * topk * 5 // (4 * expert_count)
        self.attn_cols = qc + 2 * kc
        self.slab_at = 2 * qc + 2 * kc
        self.ws_cols = self.slab_at + LANES
        self.heads = qc // HEAD_DIM
        self.group = qc // kc
        self.part_ff = ff // 4
        self.steps = n // 2


def front_kernel(
    dims,
    x, ws, g, cosine, sine, begin, routes, wg, wu, wd,
    ws_out, wg_all, wu_all, wd_all, g_all, normed, qkv, mixed, lse, resid, normed_two, coef, gates, kept,
    ws_all, scale, part, came, mid, came_far,
    ws_sems, g_sems, hid_sems, swap_sems, weight_sems, local_sems,
):
    at = Place(dims.n)
    t, d, ff4 = dims.quarter, dims.d, dims.part_ff
    q4 = d // 4
    greet((at.right, at.left), (at.sib, at.far, at.diag))

    own = local_start(ws, ws_all.at[rows_at(at.e, dims.shard)], local_sems.at[0])
    own.wait()
    ring = RingGather(
        at, lambda o, f, s: ws_all.at[pl.ds(pl.multiple_of(o * dims.shard + f, 16), s)], dims.shard, ws_sems
    )
    ring.start(0)

    swaps = Sent()
    for k, peer in enumerate((at.sib, at.far, at.diag)):
        swaps.start(
            k, remote(g.at[rows_at(peer, t)], g_all.at[at.e, :, rows_at(at.h, q4)], swap_sems, k, "hid", peer)
        )
    g_own = local_start(g.at[rows_at(at.h, t)], g_all.at[at.e, :, rows_at(at.h, q4)], local_sems.at[1])

    weights = ((wg, wg_all, 2), (wu, wu_all, 2), (wd, wd_all, 1))

    def piece(ref, dim, owner):
        spot = rows_at(owner, ff4)
        return ref.at[:, :, spot] if dim == 2 else ref.at[:, spot, :]

    moves = Sent()
    kept_own = []
    for k, (shard, whole, dim) in enumerate(weights):
        moves.start(("far", k), remote(shard, piece(whole, dim, at.h), weight_sems, k, "hid", at.far))
    for k, (shard, whole, dim) in enumerate(weights):
        moves.start(("sib", k), remote(shard, piece(whole, dim, at.h), weight_sems, 3 + k, "hid", at.sib))
        kept_own.append(local_start(shard, piece(whole, dim, at.h), local_sems.at[2 + k]))

    def pass_on(k):
        moves.recv(("far", k))
        whole, dim = weights[k][1:]
        block = piece(whole, dim, at.far)
        moves.start(("on", k), remote(block, block, weight_sems, 6 + k, "hid", at.sib))

    for j in range(4):
        rows = pl.ds(j * t, t)
        values = x[rows, :].astype(F32)
        scale[rows, :] = jnp.broadcast_to(rms(values), (t, LANES))

    for s in range(dims.steps):
        ring.recv(s)
        if s + 1 < dims.steps:
            ring.start(s + 1)
    out_ws = local_start(ws_all, ws_out, local_sems.at[5])

    for k in range(3):
        swaps.recv(k)
    g_own.wait()
    g_ring = RingGather(at, lambda o, f, s: g_all.at[o, pl.ds(f, s)], t, g_sems)
    g_ring.start(0)

    slab = ws_all[:, dims.slab_at :]
    gains = gain_rows(slab, dims.experts)
    kv = dims.kc
    for j in range(4):
        rows = pl.ds(j * t, t)
        block = (x[rows, :].astype(F32) * scale[rows, :1] * gains[0:1, :]).astype(BF16)
        normed[rows, :] = block
        raw = nn(block, ws_all[:, : dims.attn_cols])
        turned = raw[:, : dims.qc + kv]
        repeat = (dims.qc + kv) // LANES
        turned = turned * jnp.tile(cosine[rows, :], (1, repeat)) + swap_halves(turned) * jnp.tile(
            sine[rows, :], (1, repeat)
        )
        queries = turned[:, : dims.qc].astype(BF16) * jnp.asarray(HEAD_DIM**-0.5, BF16)
        qkv[rows, : dims.qc] = queries
        qkv[rows, dims.qc : dims.qc + kv] = turned[:, dims.qc :].astype(BF16)
        qkv[rows, dims.qc + kv :] = raw[:, dims.qc + kv :].astype(BF16)

    g_step = 0
    for j in range(4):
        rows = pl.ds(j * t, t)
        keys = (j + 1) * t
        bias = bias_block(begin[:, j * t : (j + 1) * t], j * t, keys)
        for head in range(dims.heads):
            key_at = dims.qc + head // dims.group * HEAD_DIM
            query = qkv[rows, head * HEAD_DIM : (head + 1) * HEAD_DIM]
            key = qkv[:keys, key_at : key_at + HEAD_DIM]
            value = qkv[:keys, key_at + kv : key_at + kv + HEAD_DIM]
            scores = nt(key, query) + bias
            peak = jnp.max(scores, axis=0, keepdims=True)
            powers = jnp.exp(scores - peak)
            total = jnp.sum(powers, axis=0, keepdims=True)
            probs = (powers * (1.0 / total)).astype(BF16)
            lse[head : head + 1, j * t : (j + 1) * t] = peak + jnp.log(total)
            mixed[rows, head * HEAD_DIM : (head + 1) * HEAD_DIM] = tn(value, probs).T.astype(BF16)
        part[j] = nt(mixed[rows, :], ws_all[:, dims.attn_cols : dims.slab_at]).astype(BF16)
        if j < 3 and g_step + 1 < dims.steps:
            g_ring.recv(g_step)
            g_step += 1
            g_ring.start(g_step)

    sums = Sent()
    sums.start(0, remote(part.at[at.diag], came.at[1], hid_sems, 0, "hid", at.sib))
    sums.start(1, remote(part.at[at.sib], came.at[0], hid_sems, 1, "hid", at.sib))
    sums.recv(0)
    mid[...] = (part[at.far].astype(F32) + came[1].astype(F32)).astype(BF16)
    sums.start(2, remote(mid, came_far, hid_sems, 2, "hid", at.far))
    sums.recv(1)

    chosen = jnp.zeros((dims.tokens, LANES), F32)
    lane = iota((dims.tokens, LANES), 1)
    for k in range(dims.topk):
        chosen = chosen + (routes[:, k : k + 1] == lane).astype(F32)
    earlier = (iota((t, dims.tokens), 1) < iota((t, dims.tokens), 0) + at.h * t).astype(BF16)
    rank = nn(earlier, chosen.astype(BF16))
    lane = iota((t, LANES), 1)
    mine = jnp.zeros((t, LANES), F32)
    route_rows = routes[rows_at(at.h, t), :]
    for k in range(dims.topk):
        mine = mine + (route_rows[:, k : k + 1] == lane).astype(F32)
    keep = mine * (rank < dims.capacity).astype(F32)
    kept[...] = keep

    sums.recv(2)
    for half in split_parts(t):
        first = pl.ds(pl.multiple_of(at.h * t + half.start, 16), half.size)
        values = (
            part[at.h, half].astype(F32) + came[0, half].astype(F32) + came_far[half].astype(F32)
            + x[first, :].astype(F32)
        )
        resid[half, :] = values
        normed_two[half, :] = (values * rms(values) * gains[1:2, :]).astype(BF16)
    logits = nn(normed_two[...], slab)
    picked = jnp.where(mine > 0, logits, NEG_FILL)
    powers = jnp.exp(picked - jnp.max(picked, axis=1, keepdims=True)) * mine
    gate = powers / jnp.sum(powers, axis=1, keepdims=True)
    gates[...] = gate
    coef[...] = (gate * keep).T[: dims.experts, :]

    while g_step + 1 < dims.steps:
        g_ring.recv(g_step)
        g_step += 1
        g_ring.start(g_step)
    for k in range(3):
        pass_on(k)
    g_ring.recv(g_step)
    for k in range(3):
        moves.recv(("sib", k))
        moves.recv(("on", k))
        kept_own[k].wait()
    out_ws.wait()
    for group in (ring, g_ring, swaps, moves, sums):
        group.done()


def moe_kernel(
    dims, big,
    x_own, coef_own, g_all, wg_in, wu_in, wd_in,
    dx, y_all, gate_grad, own_g, own_u, own_d, sib_g, sib_u, sib_d, x_far,
    x_near, g_near, coef, wg, wu, wd, d_gate, d_up, hid, send, recv, grads, stage, y_stage, x_stage, g_stage,
    x_sems, c_sems, sum_sems, grad_sems, job_sems, local_sems, keep_sems, y_sems,
):
    at = Place(dims.n)
    n, t, d, local, ff = dims.n, dims.quarter, dims.d, dims.local, dims.ff
    others = tuple((at.e + k) % n for k in range(1, n))
    greet(others, (at.sib,))

    xs = x_far if big else x_near
    coef[at.e] = coef_own[...]
    if big:
        local_start(x_own, xs.at[rows_at(at.e, t)], local_sems.at[0]).wait()
    else:
        xs[rows_at(at.e, t), :] = x_own[...]
    x_ring = RingGather(at, lambda o, f, s: xs.at[pl.ds(pl.multiple_of(o * t + f, 16), s)], t, x_sems)
    c_half = dims.experts // 2
    c_ring = RingGather(at, lambda o, f, s: coef.at[o, pl.ds(f, s)], dims.experts, c_sems)
    assert c_half % 8 == 0
    c_ring.start(0)
    x_ring.start(0)
    loads = [
        local_start(wg_in, wg, local_sems.at[1]),
        local_start(wu_in, wu, local_sems.at[2]),
        local_start(wd_in, wd, local_sems.at[3]),
    ]
    if not big:
        loads.append(local_start(g_all, g_near, local_sems.at[4]))
    for load in loads:
        load.wait()

    lane = iota((t, LANES), 1)
    y_flight = []

    def forward_row(owner, k):
        rows = rows_at(owner, t)
        if big:
            load = local_start(xs.at[rows], x_stage, local_sems.at[0])
            local_start(g_all.at[owner], g_stage, local_sems.at[4]).wait()
            load.wait()
            x_row, g_row = x_stage, g_stage
        else:
            x_row, g_row = xs.at[rows], g_near.at[owner]
        columns = jnp.concatenate(
            [coef[owner], jnp.zeros((LANES - dims.experts, t), F32)], axis=0
        ).T

        def expert(i, sums):
            share = jnp.sum(jnp.where(lane == at.e * local + i, columns, 0.0), axis=1, keepdims=True)
            pre_gate = nn(x_row[...], wg[i])
            pre_up = nn(x_row[...], wu[i])
            back = nt(g_row[...], wd[i])
            sig = 0.5 * jnp.tanh(0.5 * pre_gate) + 0.5
            silu = pre_gate * sig
            hidden = silu * pre_up
            own = jnp.sum(hidden * back, axis=1, keepdims=True)
            back = share * back
            d_up[i, rows, :] = (back * silu).astype(BF16)
            d_gate[i, rows, :] = (back * pre_up * (sig + silu * (1.0 - sig))).astype(BF16)
            hid[i, rows, :] = (share * hidden).astype(BF16)
            return jnp.where(lane == i, own, sums)

        sums = lax.fori_loop(0, local, expert, jnp.zeros((t, LANES), F32))
        grads[owner] = sums.T[:8, :]
        if len(y_flight) >= 2:
            y_flight[-2].wait()
        out = sum(nn(hid[i, rows, :], wd[i]) for i in range(local))
        y_stage[k % 2] = out.astype(BF16)
        y_flight.append(local_start(y_stage.at[k % 2], y_all.at[owner], y_sems.at[k % 2]))

    forward_row(at.e, 0)
    count = 1
    for s in range(dims.steps):
        x_ring.recv(s)
        c_ring.recv(s)
        if s + 1 < dims.steps:
            c_ring.start(s + 1)
            x_ring.start(s + 1)
        for away in (-(s + 1), s + 1) if s + 1 < dims.steps else (s + 1,):
            forward_row(at.ring(away), count)
            count += 1
    for copy in y_flight[-2:]:
        copy.wait()

    small = Sent()
    for k, peer in enumerate(others):
        small.start(k, remote(grads.at[peer], gate_grad.at[at.e], grad_sems, k, "exp", peer))
    own_small = local_start(grads.at[at.e], gate_grad.at[at.e], local_sems.at[5])

    jobs = [(kind, i) for kind in ("down", "gate", "up") for i in range(local)]
    flights = {}
    kept = {}

    def job(k):
        kind, i = jobs[k]
        slot = k % 2
        if k - 2 in flights:
            for copy in flights[k - 2]:
                copy.wait_send()
            for copy in kept[k - 2]:
                copy.wait()
        own_out, sib_out = {"down": (own_d, sib_d), "gate": (own_g, sib_g), "up": (own_u, sib_u)}[kind]
        if kind == "down":
            width = d // 2

            def strip(c, _):
                cols = rows_at(c, width)
                for f in range(ff // 256):
                    units = slice(f * 256, (f + 1) * 256)
                    if big:
                        def add(r, total):
                            rr = rows_at(r, t)
                            local_start(g_all.at[r], g_stage, local_sems.at[4]).wait()
                            return total + tn(hid[i, rr, units], g_stage[:, cols])
                        value = lax.fori_loop(0, n, add, jnp.zeros((256, width), F32))
                    else:
                        value = tn(hid[i, :, units], g_near.reshape(n * t, d)[:, cols])
                    stage[slot, c, units, :] = value.astype(BF16)
                return 0

            lax.fori_loop(0, 2, strip, 0)
            cuts = [
                (c, lambda b, c=c: stage.at[slot, c, rows_at(b, dims.part_ff), :]) for c in range(2)
            ]
            dest = lambda ref, which, c: ref.at[which, i, :, pl.ds(c * width, width)]
        else:
            grad = d_gate if kind == "gate" else d_up

            def strip(c, _):
                if big:
                    def add(r, total):
                        rr = rows_at(r, t)
                        local_start(xs.at[rr], x_stage, local_sems.at[0]).wait()
                        return total + tn(x_stage[:, rows_at(c, 256)], grad[i, rr, :])
                    value = lax.fori_loop(0, n, add, jnp.zeros((256, ff), F32))
                else:
                    value = tn(xs[:, rows_at(c, 256)], grad[i])
                stage[slot, c // 2, rows_at(c % 2, 256), :] = value.astype(BF16)
                return 0

            lax.fori_loop(0, d // 256, strip, 0)
            cuts = [
                (c, lambda b, c=c: stage.at[slot, c, :, rows_at(b, dims.part_ff)]) for c in range(2)
            ]
            dest = lambda ref, which, c: ref.at[which, i, pl.ds(c * (d // 2), d // 2), :]
        flights[k], kept[k] = [], []
        for c, cut in cuts:
            for which, block in ((1, at.diag), (0, at.sib)):
                copy = remote(cut(block), dest(sib_out, which, c), job_sems, 4 * k + 2 * c + which, "hid", at.sib)
                copy.start()
                flights[k].append(copy)
            for which, block in ((1, at.far), (0, at.h)):
                kept[k].append(
                    local_start(cut(block), dest(own_out, which, c), keep_sems.at[4 * slot + 2 * c + which])
                )

    def input_grad(owner, part):
        rows = pl.ds(pl.multiple_of(owner * t + part.start, 16), part.size)
        total = None
        for i in range(local):
            term = nt(d_gate[i, rows, :], wg[i]) + nt(d_up[i, rows, :], wu[i])
            total = term if total is None else total + term
        return total

    sums = RingSum(at, send, recv, t, sum_sems)
    done_jobs = 0
    for s in range(dims.steps):
        sums.room(s)
        for side in (0, 1):
            owner = sums.owner(s, side)
            sums.add_into(s, side, lambda part, o=owner: input_grad(o, part))
        sums.go(s)
        until = len(jobs) * (s + 1) // dims.steps
        while done_jobs < until:
            job(done_jobs)
            done_jobs += 1
    for part in split_parts(t):
        dx[part, :] = input_grad(at.e, part)
    sums.arrive_last()
    for part in split_parts(t):
        dx[part, :] = dx[part, :] + sums.total(part)

    for k in range(len(others)):
        small.recv(k)
    own_small.wait()
    for k in range(len(jobs)):
        for copy in flights[k]:
            copy.wait_recv()
        if k >= len(jobs) - 2:
            for copy in flights[k]:
                copy.wait_send()
            for copy in kept[k]:
                copy.wait()
    for group in (x_ring, c_ring, small, sums):
        group.done()


def back_kernel(
    dims, big,
    dx, gate_grad, gates, kept, resid, normed_two, g_all, x, ws, qkv, mixed, lse, normed, cosine, sine, begin,
    y_all, own_g, own_u, own_d, sib_g, sib_u, sib_d,
    layer, in_grad, small_one, small_two, att_grad, far_g, far_u, far_d,
    g_own, resid_grad, rows_all, mixed_grad, d_query, d_key, d_value, d_qkv, w_grad, part, came, mid, came_far,
    y_rows, y_send, y_recv, w_send, w_recv, out_rows, in_rows, sum_a, sum_b, cut_send, cut_recv, mid_g, mid_u, mid_d,
    row_sems, y_sems, w_sems, hid_sems, in_sems, layer_sems, small_sems, cut_sems, far_sems, local_sems,
):
    at = Place(dims.n)
    n, t, d, kv = dims.n, dims.quarter, dims.d, dims.kc
    q4 = d // 4
    others = tuple((at.e + k) % n for k in range(1, n))
    greet(others, (at.sib, at.far, at.diag))
    load_g = local_start(g_all.at[at.e], g_own, local_sems.at[0])
    if not big:
        load_y = local_start(y_all, y_rows, local_sems.at[1])
    mids = ((own_g, sib_g, mid_g, far_g), (own_u, sib_u, mid_u, far_u), (own_d, sib_d, mid_d, far_d))
    loads = []
    for k, (own, sib, one, _) in enumerate(mids):
        loads.append(local_start(own.at[1], one.at[0], local_sems.at[2 + 2 * k]))
        loads.append(local_start(sib.at[1], one.at[1], local_sems.at[3 + 2 * k]))

    slab = ws[:, dims.slab_at :]
    gains = gain_rows(slab, dims.experts)
    spread_shape = (n * 8, LANES)
    sub, lane = iota(spread_shape, 0), iota(spread_shape, 1)
    spread = (
        (sub // 8 == lane // dims.local) & (sub % 8 == lane % dims.local) & (lane < dims.experts)
    ).astype(F32)
    gg = tn_exact(gate_grad[...], spread) * kept[...]
    gate = gates[...]
    logit_grad = (gate * (gg - jnp.sum(gate * gg, axis=1, keepdims=True))).astype(BF16)
    load_g.wait()
    gain_two = jnp.zeros((1, d), F32)
    for half in split_parts(t):
        lg = logit_grad[half.start : half.start + half.size, :]
        normed_grad = dx[half, :] + nt(lg, slab)
        inputs = resid[half, :]
        scale = rms(inputs)
        gain_two = gain_two + jnp.sum(normed_grad * inputs * scale, axis=0, keepdims=True)
        weighted = normed_grad * gains[1:2, :]
        value = (
            g_own[half, :].astype(F32) + scale * weighted
            - inputs * (scale * scale * scale) * jnp.mean(weighted * inputs, axis=-1, keepdims=True)
        )
        resid_grad[half, :] = value
        rows_all[pl.ds(pl.multiple_of(at.h * t + half.start, 16), half.size), :] = value.astype(BF16)

    rows = Sent()
    mine = rows_all.at[rows_at(at.h, t)]
    rows.start(0, remote(mine, mine, row_sems, 0, "hid", at.far))
    rows.start(1, remote(mine, mine, row_sems, 1, "hid", at.sib))

    router_rows = dims.experts
    small_rows = router_rows + 8
    sum_a[0, :router_rows, :] = tn(logit_grad, normed_two[...])[:router_rows, :]
    sum_a[0, router_rows:, :] = jnp.broadcast_to(gain_two, (8, d))
    smalls = Sent()
    smalls.start(0, remote(sum_a.at[0], sum_a.at[1], small_sems, 0, "hid", at.sib))

    if not big:
        load_y.wait()
    y_sum = RingSum(at, y_send, y_recv, t, y_sems)

    def y_row(owner):
        if not big:
            return y_rows.at[owner]
        local_start(y_all.at[owner], y_rows.at[0], local_sems.at[1]).wait()
        return y_rows.at[0]

    def y_step(s):
        y_sum.room(s)
        for side in (0, 1):
            row = y_row(y_sum.owner(s, side))
            y_sum.add_into(s, side, lambda part, row=row: row[part].astype(F32))
        y_sum.go(s)

    y_step(0)

    smalls.recv(0)
    sum_a[2] = sum_a[0] + sum_a[1]
    smalls.start(1, remote(sum_a.at[2], sum_a.at[3], small_sems, 1, "hid", at.far))

    rows.recv(0)
    theirs = rows_all.at[rows_at(at.far, t)]
    rows.start(2, remote(theirs, theirs, row_sems, 2, "hid", at.sib))
    for load in loads:
        load.wait()
    fars = Sent()
    for k, (_, _, one, far) in enumerate(mids):
        def add(i, _, one=one):
            one[0, i] = (one[0, i].astype(F32) + one[1, i].astype(F32)).astype(BF16)
            return 0
        lax.fori_loop(0, dims.local, add, 0)
    rows.recv(1)
    rows.recv(2)

    wo = ws[:, dims.attn_cols : dims.slab_at]
    for j in range(4):
        block = pl.ds(j * t, t)
        mixed_grad[block, :] = nn(rows_all[block, :], wo).astype(BF16)
    for k, (_, _, one, far) in enumerate(mids):
        fars.start(k, remote(one.at[0], far, far_sems, k, "hid", at.far))

    shard = dims.shard
    smalls.recv(1)
    sum_a[1] = sum_a[2] + sum_a[3]
    cuts = Sent()
    for owner in range(n):
        cut_send[owner, :small_rows] = sum_a[1, :, owner * shard : (owner + 1) * shard]
    for k, peer in enumerate(others):
        cuts.start(
            k,
            remote(
                cut_send.at[peer, pl.ds(0, small_rows)], cut_recv.at[at.e, pl.ds(0, small_rows)], cut_sems, k, "exp", peer
            ),
        )
    own_cut = local_start(
        cut_send.at[at.e, pl.ds(0, small_rows)], cut_recv.at[at.e, pl.ds(0, small_rows)], local_sems.at[8]
    )

    d_key[...] = jnp.zeros_like(d_key)
    d_value[...] = jnp.zeros_like(d_value)
    y_at = 1
    for j in range(4):
        block = pl.ds(j * t, t)
        keys = (j + 1) * t
        bias = bias_block(begin[:, j * t : (j + 1) * t], j * t, keys)
        for head in range(dims.heads):
            key_at = head // dims.group * HEAD_DIM
            spot = slice(key_at, key_at + HEAD_DIM)
            query = qkv[block, head * HEAD_DIM : (head + 1) * HEAD_DIM]
            key = qkv[:keys, dims.qc + key_at : dims.qc + key_at + HEAD_DIM]
            value = qkv[:keys, dims.qc + kv + key_at : dims.qc + kv + key_at + HEAD_DIM]
            out_grad = mixed_grad[block, head * HEAD_DIM : (head + 1) * HEAD_DIM]
            probs = jnp.exp(nt(key, query) + bias - lse[head : head + 1, j * t : (j + 1) * t])
            prob_grad = nt(value, out_grad)
            inner = jnp.sum(probs * prob_grad, axis=0, keepdims=True)
            score_grad = (probs * (prob_grad - inner)).astype(BF16)
            d_query[block, head * HEAD_DIM : (head + 1) * HEAD_DIM] = tn(score_grad, key) * HEAD_DIM**-0.5
            d_key[:keys, spot] += nn(score_grad, query)
            d_value[:keys, spot] += nn(probs.astype(BF16), out_grad)
        if y_at < dims.steps:
            y_step(y_at)
            y_at += 1

    for j in range(4):
        block = pl.ds(j * t, t)
        raw = jnp.concatenate([d_query[block, :], d_key[block, :]], axis=1)
        repeat = (dims.qc + kv) // LANES
        turned = raw * jnp.tile(cosine[block, :], (1, repeat)) - swap_halves(raw) * jnp.tile(
            sine[block, :], (1, repeat)
        )
        d_qkv[block, : dims.qc + kv] = turned.astype(BF16)
        d_qkv[block, dims.qc + kv :] = d_value[block, :].astype(BF16)
        part[j] = nt(d_qkv[block, :], ws[:, : dims.attn_cols]).astype(BF16)

    sums = Sent()
    sums.start(0, remote(part.at[at.diag], came.at[1], hid_sems, 0, "hid", at.sib))
    sums.start(1, remote(part.at[at.sib], came.at[0], hid_sems, 1, "hid", at.sib))
    for c in range(d // 256):
        cols = slice(c * 256, (c + 1) * 256)
        w_grad[cols, : dims.attn_cols] = tn(normed[:, cols], d_qkv[...])
        w_grad[cols, dims.attn_cols :] = tn(rows_all[:, cols], mixed[...])
    sums.recv(0)
    mid[...] = (part[at.far].astype(F32) + came[1].astype(F32)).astype(BF16)
    sums.start(2, remote(mid, came_far, hid_sems, 2, "hid", at.far))
    sums.recv(1)

    w_sum = RingSum(at, w_send, w_recv, shard, w_sems)

    def w_step(s):
        w_sum.room(s)
        for side in (0, 1):
            owner = w_sum.owner(s, side)
            w_sum.add_into(
                s, side, lambda part, o=owner: w_grad[pl.ds(pl.multiple_of(o * shard + part.start, 16), part.size), :]
            )
        w_sum.go(s)

    w_step(0)
    while y_at < dims.steps:
        y_step(y_at)
        y_at += 1
    y_sum.arrive_last()
    y_own = y_row(at.e)
    for half in split_parts(t):
        out_rows[half, :] = (
            resid[half, :] + y_own[half].astype(F32) + y_sum.total(half)
        ).astype(BF16)
    layers = Sent()

    sums.recv(2)
    gain_one = jnp.zeros((1, d), F32)
    for half in split_parts(t):
        here = pl.ds(pl.multiple_of(at.h * t + half.start, 16), half.size)
        grad = part[at.h, half].astype(F32) + came[0, half].astype(F32) + came_far[half].astype(F32)
        inputs = x[here, :].astype(F32)
        scale = rms(inputs)
        gain_one = gain_one + jnp.sum(grad * inputs * scale, axis=0, keepdims=True)
        weighted = grad * gains[0:1, :]
        in_rows[half, :] = (
            resid_grad[half, :] + scale * weighted
            - inputs * (scale * scale * scale) * jnp.mean(weighted * inputs, axis=-1, keepdims=True)
        ).astype(BF16)
    ins = Sent()
    spot = in_grad.at[rows_at(at.h, t)]
    ins.start(0, remote(in_rows, spot, in_sems, 0, "hid", at.far))
    ins.start(1, remote(in_rows, spot, in_sems, 1, "hid", at.sib))
    own_in = local_start(in_rows, spot, local_sems.at[9])
    sum_b[0] = jnp.broadcast_to(gain_one, (8, d))
    smalls.start(2, remote(sum_b.at[0], sum_b.at[1], small_sems, 2, "hid", at.sib))
    for k, peer in enumerate((at.sib, at.far, at.diag)):
        layers.start(
            k, remote(out_rows.at[:, rows_at(peer, q4)], layer.at[rows_at(at.h, t)], layer_sems, k, "hid", peer)
        )
    own_layer = local_start(out_rows.at[:, rows_at(at.h, q4)], layer.at[rows_at(at.h, t)], local_sems.at[10])
    smalls.recv(2)
    sum_b[2] = sum_b[0] + sum_b[1]
    smalls.start(3, remote(sum_b.at[2], sum_b.at[3], small_sems, 3, "hid", at.far))
    w_at = 1
    if w_at < dims.steps:
        w_step(w_at)
        w_at += 1
    smalls.recv(3)
    sum_b[1] = sum_b[2] + sum_b[3]
    for owner in range(n):
        cut_send[owner, small_rows:] = sum_b[1, :, owner * shard : (owner + 1) * shard]
    for k, peer in enumerate(others):
        cuts.start(
            n + k,
            remote(
                cut_send.at[peer, pl.ds(small_rows, 8)], cut_recv.at[at.e, pl.ds(small_rows, 8)], cut_sems, n - 1 + k, "exp",
                peer,
            ),
        )
    own_cut_two = local_start(
        cut_send.at[at.e, pl.ds(small_rows, 8)], cut_recv.at[at.e, pl.ds(small_rows, 8)], local_sems.at[11]
    )
    ins.recv(0)
    far_rows = in_grad.at[rows_at(at.far, t)]
    ins.start(2, remote(far_rows, far_rows, in_sems, 2, "hid", at.sib))
    while w_at < dims.steps:
        w_step(w_at)
        w_at += 1
    w_sum.arrive_last()
    for part_rows in split_parts(shard):
        here = pl.ds(pl.multiple_of(at.e * shard + part_rows.start, 16), part_rows.size)
        att_grad[part_rows, :] = w_grad[here, :] + w_sum.total(part_rows)

    for k in range(n - 1):
        cuts.recv(k)
        cuts.recv(n + k)
    own_cut.wait()
    own_cut_two.wait()
    total = cut_recv[0]
    for k in range(1, n):
        total = total + cut_recv[k]
    small_one[...] = total[:small_rows]
    small_two[...] = total[small_rows:]

    for k in range(3):
        fars.recv(k)
        layers.recv(k)
    ins.recv(1)
    ins.recv(2)
    own_in.wait()
    own_layer.wait()
    for group in (rows, smalls, y_sum, fars, cuts, sums, w_sum, ins, layers):
        group.done()


def tables(segments, token_count):
    counts = [jnp.sum((segments == k).astype(jnp.int32)) for k in range(SEGS)]
    begin = jnp.zeros((token_count,), jnp.int32)
    start = jnp.zeros((), jnp.int32)
    for k in range(SEGS):
        begin = begin + jnp.where(segments == k, start, 0)
        start = start + counts[k]
    positions = jnp.arange(token_count, dtype=jnp.int32) - begin
    half = HEAD_DIM // 2
    freqs = ROPE_BASE ** (-(jnp.arange(half, dtype=F32) * 2.0 / HEAD_DIM))
    angles = positions.astype(F32)[:, None] * freqs[None, :]
    cosine, sine = jnp.cos(angles), jnp.sin(angles)
    return begin[None, :], jnp.concatenate([cosine] * 4, axis=1), jnp.concatenate([-sine, sine] * 2, axis=1)


def per_device(
    tokens,
    segment_ids,
    routes,
    norm1_gain,
    norm2_gain,
    query_weight,
    key_matrix,
    value_matrix,
    out_weight,
    router_weight,
    gate_weight,
    up_weight,
    down_weight,
    out_grad,
):
    n = lax.axis_size("exp")
    assert lax.axis_size("hid") == 4
    token_count, d = tokens.shape
    local, _, part_ff = gate_weight.shape
    experts = router_weight.shape[1]
    dims = Dims(
        n, token_count, d, experts, local, 4 * part_ff, routes.shape[1], query_weight.shape[1], key_matrix.shape[1]
    )
    t, ff, steps, shard = dims.quarter, dims.ff, dims.steps, dims.shard
    begin, cosine, sine = tables(segment_ids[0], token_count)
    pad = jnp.zeros((shard, LANES - experts - 2), F32)
    ws = jnp.concatenate(
        [query_weight, key_matrix, value_matrix, out_weight, router_weight, norm1_gain[:, None], norm2_gain[:, None], pad],
        axis=1,
    ).astype(BF16)
    wg, wu, wd = gate_weight.astype(BF16), up_weight.astype(BF16), down_weight.astype(BF16)

    vmem = pl.BlockSpec(memory_space=pltpu.VMEM)
    anywhere = pl.BlockSpec(memory_space=pl.ANY)
    shape = jax.ShapeDtypeStruct
    dma = pltpu.SemaphoreType.DMA

    (ws_all, wg_all, wu_all, wd_all, g_all, normed, qkv, mixed, lse, resid, normed_two, coef, gates, kept) = pl.pallas_call(
        functools.partial(front_kernel, dims),
        out_shape=[
            shape((d, dims.ws_cols), BF16),
            shape((local, d, ff), BF16),
            shape((local, d, ff), BF16),
            shape((local, ff, d), BF16),
            shape((n, t, d), BF16),
            shape((token_count, d), BF16),
            shape((token_count, dims.attn_cols), BF16),
            shape((token_count, dims.qc), BF16),
            shape((8, token_count), F32),
            shape((t, d), F32),
            shape((t, d), BF16),
            shape((experts, t), F32),
            shape((t, LANES), F32),
            shape((t, LANES), F32),
        ],
        in_specs=[vmem, vmem, anywhere, vmem, vmem, vmem, vmem, anywhere, anywhere, anywhere],
        out_specs=[anywhere] * 5 + [vmem] * 9,
        scratch_shapes=[
            pltpu.VMEM((d, dims.ws_cols), BF16),
            pltpu.VMEM((token_count, LANES), F32),
            pltpu.VMEM((4, t, d), BF16),
            pltpu.VMEM((2, t, d), BF16),
            pltpu.VMEM((t, d), BF16),
            pltpu.VMEM((t, d), BF16),
            dma((2, 2 * steps)),
            dma((2, 2 * steps)),
            dma((2, 3)),
            dma((2, 3)),
            dma((2, 9)),
            dma((6,)),
        ],
        compiler_params=pltpu.CompilerParams(
            collective_id=0, has_side_effects=True, vmem_limit_bytes=SMALL_VMEM
        ),
    )(tokens, ws, out_grad, cosine, sine, begin, routes, wg, wu, wd)

    big = n * t * d * 2 > 6 * 2**20
    near = 16 if big else n * t
    jobs = 3 * local
    wide = [shape((2, local, d, part_ff), BF16)] * 2 + [shape((2, local, part_ff, d), BF16)]
    (dx, y_all, gate_grad, own_g, own_u, own_d, sib_g, sib_u, sib_d, _) = pl.pallas_call(
        functools.partial(moe_kernel, dims, big),
        out_shape=[shape((t, d), F32), shape((n, t, d), BF16), shape((n, 8, t), F32)]
        + wide
        + wide
        + [shape((n * t if big else 16, d), BF16)],
        in_specs=[vmem, vmem] + [anywhere] * 4,
        out_specs=[vmem] + [anywhere] * 9,
        scratch_shapes=[
            pltpu.VMEM((near, d), BF16),
            pltpu.VMEM((1, 16, d) if big else (n, t, d), BF16),
            pltpu.VMEM((n, experts, t), F32),
            pltpu.VMEM((local, d, ff), BF16),
            pltpu.VMEM((local, d, ff), BF16),
            pltpu.VMEM((local, ff, d), BF16),
            pltpu.VMEM((local, n * t, ff), BF16),
            pltpu.VMEM((local, n * t, ff), BF16),
            pltpu.VMEM((local, n * t, ff), BF16),
            pltpu.VMEM((2, 2, t, d), BF16),
            pltpu.VMEM((2, steps, t, d), BF16),
            pltpu.VMEM((n, 8, t), F32),
            pltpu.VMEM((2, 2, d // 2, ff), BF16),
            pltpu.VMEM((2, t, d), BF16),
            pltpu.VMEM((t, d) if big else (16, LANES), BF16),
            pltpu.VMEM((t, d) if big else (16, LANES), BF16),
            dma((2, 2 * steps)),
            dma((2, 2 * steps)),
            dma((2, 2 * steps)),
            dma((2, n - 1)),
            dma((2, 4 * jobs)),
            dma((6,)),
            dma((8,)),
            dma((2,)),
        ],
        compiler_params=pltpu.CompilerParams(
            collective_id=1, has_side_effects=True, vmem_limit_bytes=VMEM_LIMIT
        ),
    )(normed_two, coef, g_all, wg_all, wu_all, wd_all)

    small_rows = experts + 8
    att = dims.attn_cols + dims.qc
    (layer, in_grad, small_one, small_two, att_grad, far_g, far_u, far_d) = pl.pallas_call(
        functools.partial(back_kernel, dims, big),
        out_shape=[
            shape((token_count, d // 4), BF16),
            shape((token_count, d), BF16),
            shape((small_rows, shard), F32),
            shape((8, shard), F32),
            shape((shard, att), F32),
            shape((local, d, part_ff), BF16),
            shape((local, d, part_ff), BF16),
            shape((local, part_ff, d), BF16),
        ],
        in_specs=[vmem] * 6 + [anywhere] + [vmem] * 9 + [anywhere] * 7,
        out_specs=[anywhere] * 2 + [vmem] * 3 + [anywhere] * 3,
        scratch_shapes=[
            pltpu.VMEM((t, d), BF16),
            pltpu.VMEM((t, d), F32),
            pltpu.VMEM((token_count, d), BF16),
            pltpu.VMEM((token_count, dims.qc), BF16),
            pltpu.VMEM((token_count, dims.qc), F32),
            pltpu.VMEM((token_count, dims.kc), F32),
            pltpu.VMEM((token_count, dims.kc), F32),
            pltpu.VMEM((token_count, dims.attn_cols), BF16),
            pltpu.VMEM((d, att), F32),
            pltpu.VMEM((4, t, d), BF16),
            pltpu.VMEM((2, t, d), BF16),
            pltpu.VMEM((t, d), BF16),
            pltpu.VMEM((t, d), BF16),
            pltpu.VMEM((1 if big else n, t, d), BF16),
            pltpu.VMEM((2, 2, t, d), BF16),
            pltpu.VMEM((2, steps, t, d), BF16),
            pltpu.VMEM((2, 2, shard, att), BF16),
            pltpu.VMEM((2, steps, shard, att), BF16),
            pltpu.VMEM((t, d), BF16),
            pltpu.VMEM((t, d), BF16),
            pltpu.VMEM((4, small_rows, d), F32),
            pltpu.VMEM((4, 8, d), F32),
            pltpu.VMEM((n, small_rows + 8, shard), F32),
            pltpu.VMEM((n, small_rows + 8, shard), F32),
            pltpu.VMEM((2, local, d, part_ff), BF16),
            pltpu.VMEM((2, local, d, part_ff), BF16),
            pltpu.VMEM((2, local, part_ff, d), BF16),
            dma((2, 3)),
            dma((2, 2 * steps)),
            dma((2, 2 * steps)),
            dma((2, 3)),
            dma((2, 3)),
            dma((2, 3)),
            dma((2, 4)),
            dma((2, 2 * (n - 1))),
            dma((2, 3)),
            dma((12,)),
        ],
        compiler_params=pltpu.CompilerParams(
            collective_id=2, has_side_effects=True, vmem_limit_bytes=VMEM_LIMIT
        ),
    )(
        dx, gate_grad.reshape(n * 8, t), gates, kept, resid, normed_two, g_all, tokens, ws_all, qkv, mixed, lse, normed,
        cosine, sine, begin, y_all, own_g, own_u, own_d, sib_g, sib_u, sib_d,
    )

    def three(own, sib, far):
        return own[0].astype(F32) + sib[0].astype(F32) + far.astype(F32)

    qc, kc = dims.qc, dims.kc
    return (
        layer,
        in_grad.astype(F32),
        small_two[0],
        small_one[experts],
        att_grad[:, :qc],
        att_grad[:, qc : qc + kc],
        att_grad[:, qc + kc : qc + 2 * kc],
        att_grad[:, dims.attn_cols :],
        small_one[:experts].T,
        three(own_g, sib_g, far_g),
        three(own_u, sib_u, far_u),
        three(own_d, sib_d, far_d),
    )


def solution(mesh):
    in_specs = (
        P("exp", None),
        P("exp", None),
        P("exp", None),
        P("exp"),
        P("exp"),
        P("exp", "hid"),
        P("exp", "hid"),
        P("exp", "hid"),
        P("exp", "hid"),
        P("exp", None),
        P("exp", None, "hid"),
        P("exp", None, "hid"),
        P("exp", "hid", None),
        P("exp", "hid"),
    )
    out_specs = (
        P("exp", "hid"),
        P("exp", None),
        P("exp"),
        P("exp"),
        P("exp", "hid"),
        P("exp", "hid"),
        P("exp", "hid"),
        P("exp", "hid"),
        P("exp", None),
        P("exp", None, "hid"),
        P("exp", None, "hid"),
        P("exp", "hid", None),
    )
    return jax.shard_map(
        per_device, mesh=mesh, in_specs=in_specs, out_specs=out_specs, check_vma=False
    )
```

time: 2180 us -> 437 us (0.20)
  waiting for transfers between devices: 1240 us -> 0 us
  Pallas kernels: 0 us -> 385 us
  local copies, waits for them, and re-layouts: 287 us -> 21.8 us
  matrix products: 220 us -> 0 us
  blocking collectives: 216 us -> 0 us
  other arithmetic: 105 us -> 22.5 us
  starting transfers between devices: 76.1 us -> 0 us
    all_to_all x4 -> x0, waiting for transfers between devices: 648 us -> none  [the longest x1 379 us: per_device(): lax.all_to_all(outgoing, 'exp', split_axis=0, concat_axis=0, tiled=True)]
    reduce_scatter x6 -> x0, waiting for transfers between devices: 540 us -> none  [the longest x1 259 us: per_device(): lax.psum_scatter(slot_input, 'hid', scatter_dimension=3, tiled=True)]
    pallas_call x0 -> x3, Pallas kernels: none -> 385 us  [the longest x1 150 us: per_device(): pl.pallas_call(functools.partial(moe_kernel, dims, big), out_shape=[shape...]
    dot_general x38 -> x0, matrix products: 220 us -> none  [the longest x1 28.3 us: per_device(): jnp.einsum('secf,edf->secd', pre_up_grad, up_use, preferred_element_type=...]
    all_gather x8 -> x0, blocking collectives: 194 us -> none  [the longest x1 31.5 us: per_device(): lax.all_gather(out_weight.astype(jnp.bfloat16), 'exp', axis=0, tiled=True)]
    gather x4 -> x0, local copies, waits for them, and re-layouts: 154 us -> none  [the longest x1 44.1 us: per_device(): outgoing = padded[source].reshape(expert_count, capacity, model_width)]
    all_to_all x4 -> x0, starting transfers between devices: 75.4 us -> none  [the longest x1 59.5 us: per_device(): lax.all_to_all(outgoing, 'exp', split_axis=0, concat_axis=0, tiled=True)]
    scatter x2 -> x0, local copies, waits for them, and re-layouts: 60.9 us -> none  [the longest x1 30.5 us: slot_tables(): source = source.at[pair_slot.reshape(-1)].set(owners.reshape(-1))]
  transfers between devices with their start and end apart: 16 -> 0, of which waited for: 10 -> 0; matrix products, arithmetic and copies ran while one was open for 21% -> 0% of each run, Pallas kernels for 0% -> 0%
where the time goes in v1:
time: 437 us; the launch traced here: 432 us
  Pallas kernels  385 us (88%)
  other arithmetic  22.5 us (5%)
  local copies, waits for them, and re-layouts  21.8 us (5%)
    pallas_call x1, Pallas kernels, per_device(): pl.pallas_call(functools.partial(moe_kernel, dims, big), out_shape=[shape...  150 us
    pallas_call x1, Pallas kernels, per_device(): pl.pallas_call(functools.partial(back_kernel, dims, big), out_shape=[shap...  138 us
    pallas_call x1, Pallas kernels, per_device(): pl.pallas_call(functools.partial(front_kernel, dims), out_shape=[shape((d...  96.6 us
    unnamed x62, local copies, waits for them, and re-layouts  17.6 us

profile of v1, /device:TPU:0, one launch (start us, length us, event | category | flops | bytes accessed | tf_op | source)
XLA Modules:
  0.0 432.3 jit_solution(7009512735379199545)
XLA Ops:
  0.6 0.7 convert_bitcast_fusion.1
  1.3 0.7 convert_bitcast_fusion
  2.0 1.4 fusion.4
  5.3 1.3 fusion.2.begin
  6.7 0.7 convert.29
  7.4 0.1 copy.30
  7.5 0.1 copy.32
  7.6 0.1 copy.31
  7.8 0.9 convert.26
  8.6 0.8 convert.27
  9.5 0.9 convert.25
  10.4 0.9 convert.28
  11.3 0.1 concatenate.10.ws
  11.5 1.1 copy.34.routes
  12.5 1.7 convert_element_type.69.wg
  14.3 0.1 convert_element_type.70.wu
  14.5 1.4 copy-done.24
  15.9 0.1 convert_element_type.71.wd
  16.1 1.9 fusion
  18.0 0.9 pad_maximum_fusion
  18.9 96.6 %shard_map.229 = (bf16[1024,896]{1,0:T(8,128)(2,1)S(1)}, bf16[4,1024,512]{2,1,0:T(8,128)(2,1)S(1)}, bf16[4,1024,512]{2,1,0:T(8,128)(2,1)S(1)}, bf16[4,512,1024]{...) custom-call(bf16[1024,1024]{1,0:T(8,128)(2,1)S(1)} %copy-done, ...), custom_call_target="tpu_custom_call" | custom-call | tf_op jit(solution)/shard_map/pallas_call | solution.py:932
  115.6 2.0 copy-done.3
  117.6 1.9 copy-done.4
  119.5 0.8 copy-done.5
  120.3 1.3 copy-done.6
  121.6 1.2 copy-done.7
  122.8 1.0 copy-done.8
  123.9 1.0 copy-done.9
  124.8 0.8 copy-done.10
  125.7 0.7 copy-done.12
  126.3 0.7 copy-done.13
  127.0 0.6 copy-done.15
  127.6 0.6 copy-done.16
  128.2 150.1 %shard_map.230 = (f32[256,1024]{1,0:T(8,128)}, bf16[8,256,1024]{2,1,0:T(8,128)(2,1)}, f32[8,8,256]{2,1,0:T(8,128)}, bf16[2,4,1024,128]{3,2,1,0:T(8,128)(2,1)}, b...) custom-call(bf16[256,1024]{1,0:T(8,128)(2,1)} %copy-done.5, ...), custom_call_target="tpu_custom_call" | custom-call | tf_op jit(solution)/shard_map/pallas_call | solution.py:975
  278.4 138.2 %shard_map.231 = (bf16[1024,256]{1,0:T(8,128)(2,1)}, bf16[1024,1024]{1,0:T(8,128)(2,1)}, f32[40,128]{1,0:T(8,128)}, f32[8,128]{1,0:T(8,128)}, f32[128,768]{1,0:T...) custom-call(f32[256,1024]{1,0:T(8,128)} %get-tuple-element.49.dx, ...), custom_call_target="tpu_custom_call" | custom-call | tf_op jit(solution)/shard_map/pallas_call | solution.py:1016
  416.6 3.6 bitcast_add_fusion
  420.2 1.7 bitcast_add_fusion.1
  421.9 0.5 copy-done.17
  422.4 0.8 copy-done.18
  423.2 0.3 copy-done.25
  423.4 1.7 bitcast_add_fusion.2
  425.1 1.2 slice_bitcast_fusion.2
  426.3 0.5 slice_bitcast_fusion.1
  426.8 0.6 slice_bitcast_fusion
  427.4 0.7 fusion.7
  428.1 0.7 fusion.6
  428.8 2.5 convert_element_type.72
  431.3 0.8 copy.36
  (47 shorter events, 0.1 us)
Async XLA Ops:
  6.6 12.2 %copy-start.14 = (s32[1,1024]{1,0:T(1,128)}, s32[1,1024]{1,0:T(1,128)S(1)}, u32[]{:S(2)}) copy-start(s32[1,1024]{1,0:T(1,128)S(1)} %fusion.2.begin) | copy-start | bytes 12292
  11.3 3.0 copy-start.23
  14.3 1.6 copy-start.24
  16.0 2.8 copy-start
  16.1 2.8 copy-start.11
  18.9 96.7 %copy-start.1 = (f32[1024,128]{1,0:T(8,128)}, f32[1024,128]{1,0:T(8,128)S(1)}, u32[]{:S(2)}) copy-start(f32[1024,128]{1,0:T(8,128)S(1)} %get-tuple-element.84.cosine) | copy-start | bytes 1572868
  18.9 96.7 %copy-start.2 = (f32[1024,128]{1,0:T(8,128)}, f32[1024,128]{1,0:T(8,128)S(1)}, u32[]{:S(2)}) copy-start(f32[1024,128]{1,0:T(8,128)S(1)} %get-tuple-element.85.sine) | copy-start | bytes 1572868
  115.6 2.0 copy-start.3
  117.6 1.9 copy-start.4
  119.5 0.8 copy-start.5
  120.3 1.3 copy-start.6
  121.6 1.2 copy-start.7
  122.8 1.0 copy-start.8
  123.9 1.0 copy-start.9
  124.8 0.8 copy-start.10
  125.7 0.7 copy-start.12
  126.3 0.7 copy-start.13
  127.0 0.6 copy-start.15
  127.6 0.6 copy-start.16
  278.3 138.2 %copy-start.21 = (bf16[2,4,128,1024]{3,2,1,0:T(8,128)(2,1)S(1)}, bf16[2,4,128,1024]{3,2,1,0:T(8,128)(2,1)}, u32[]{:S(2)}) copy-start(bf16[2,4,128,1024]{3,2,1,0:T(8,128)(2,1)} %get-tuple-element.62.own_d) | copy-start | bytes 6291460
  416.5 3.7 copy-start.19
  416.5 3.6 copy-start.20
  416.5 3.6 copy-start.26
  420.2 2.2 copy-start.17
  420.2 3.0 copy-start.18
  420.2 3.2 copy-start.25
  423.4 2.9 copy-start.29
  423.4 4.0 copy-start.28
  423.4 5.4 %copy-start.22 = (bf16[1024,1024]{1,0:T(8,128)(2,1)S(1)}, bf16[1024,1024]{1,0:T(8,128)(2,1)}, u32[]{:S(2)}) copy-start(bf16[1024,1024]{1,0:T(8,128)(2,1)} %get-tuple-element.67) | copy-start | bytes 6291460
  428.8 2.5 copy-start.27
